TPU v7x, 128 devices: a whole 4x4x4 slice. The times are simulated.
128 devices in a mesh: tm: 32 (over x, z, core), row: 4 (over y).
Axes of the slice: x: 4, y: 4, z: 4, core: 2. Of those that a mesh axis runs over, the one named last changes fastest.
Arguments:
- gain_mats: bfloat16 [32, 1024, 1024], P('tm', 'row'), may hold values from -1 to 1
- offsets: bfloat16 [32, 1024], P('tm', 'row'), may hold values from -1.796875 to 1.796875
- spread_mats: bfloat16 [32, 1024, 1024], P('tm', 'row'), may hold values from -1 to 8, as said below
Outputs:
- smoothed_mean: bfloat16 [32, 1024], P('tm', 'row')
- smoothed_cov: bfloat16 [32, 1024, 1024], P('tm', 'row')
Inputs may be any that keep to these rules, and one draw needn't show every extreme that they name: `spread_mats`: symmetric.
All inputs are finite; a program needn't handle non-finite values.
Results may differ from a plain program's by a relative error of at most 0.0035.
The roundings to bfloat16 on the way count: a program that leaves them out, or rounds other values in their place, can miss the bound.
Values may be sent and summed in bfloat16 or wider, within the bound.
A program may use at most 64 MiB of HBM per device.

v0:
```python
import jax
import jax.numpy as jnp
from jax import lax
from jax.sharding import PartitionSpec as P


def for_sending(shard):
    return jax.tree.map(lambda a: a.astype(jnp.bfloat16) if a.dtype == jnp.float32 else a, shard)


def passed_along(block, axis, distance):
    devices = range(lax.axis_size(axis))
    route = [(i - distance, i) for i in devices if i - distance in devices]
    return lax.ppermute(block, axis, route)


def compose(own_gain, own_offset, own_spread, gain_whole, far_gain, far_offset, far_spread):
    new_gain = jnp.dot(own_gain[0], far_gain[0], preferred_element_type=jnp.float32).astype(
        jnp.bfloat16
    )
    new_offset = (
        jnp.dot(own_gain[0], far_offset[0], preferred_element_type=jnp.float32)
        + own_offset[0].astype(jnp.float32)
    ).astype(jnp.bfloat16)
    middle = jnp.dot(own_gain[0], far_spread[0], preferred_element_type=jnp.float32).astype(
        jnp.bfloat16
    )
    outer = lax.dot_general(
        middle, gain_whole[0], (((1,), (1,)), ((), ())), preferred_element_type=jnp.float32
    )
    new_spread = (outer + own_spread[0].astype(jnp.float32)).astype(jnp.bfloat16)
    return (new_gain[None], new_offset[None], new_spread[None])


def per_device(gain_mats, offsets, spread_mats):
    tm_count = lax.axis_size("tm")
    tm_index = lax.axis_index("tm")
    levels = tm_count.bit_length() - 1
    first_gain = jnp.where(tm_index == tm_count - 1, jnp.zeros_like(gain_mats), gain_mats)
    own_part = (first_gain, offsets, spread_mats)
    whole_rows = (
        lax.all_gather(own_part[0], "row", axis=1, tiled=True),
        lax.all_gather(own_part[1], "row", axis=1, tiled=True),
        lax.all_gather(own_part[2], "row", axis=1, tiled=True),
    )
    for level in range(levels):
        distance = 1 << level
        far_part = jax.tree.map(
            lambda part, own: part.astype(own.dtype),
            passed_along(for_sending(whole_rows), "tm", -distance),
            whole_rows,
        )
        result = compose(
            own_part[0],
            own_part[1],
            own_part[2],
            whole_rows[0],
            far_part[0],
            far_part[1],
            far_part[2],
        )
        is_valid = tm_index + distance < tm_count
        own_part = tuple(
            (jnp.where(is_valid, fresh, older) for fresh, older in zip(result, own_part))
        )
        if level + 1 < levels:
            whole_rows = jax.tree.map(
                lambda part, own: part.astype(own.dtype),
                lax.all_gather(for_sending(own_part), "row", axis=1, tiled=True),
                own_part,
            )
    return (own_part[1], own_part[2])


def solution(mesh):
    in_specs = (P("tm", "row", None), P("tm", "row"), P("tm", "row", None))
    out_specs = (P("tm", "row"), P("tm", "row", None))
    return jax.shard_map(
        per_device, mesh=mesh, in_specs=in_specs, out_specs=out_specs, check_vma=False
    )
```

profile of v0, /device:TPU:66, one launch (start us, length us, event | category | flops | bytes accessed | tf_op | source)
XLA Modules:
  0.0 526.5 jit_solution(14572666628458016894)
XLA Ops:
  9.9 32.3 %all-gather.19.cloned.1.call-done = bf16[1,1024,1024]{2,1,0:T(8,128)(2,1)} async-done(((bf16[1,256,1024]{2,1,0:T(8,128)(2,1)}), bf16[1,1024,1024]{2,1,0:T(8,128)(2,1)}) %all-gather.19.cloned.1.call-update) | async-done | bytes 2097168 | tf_op jit(solution)/shard_map/all_gather | solution.py:44
  44.1 31.2 %all-gather.11.cloned.1.call-done = bf16[1,1024,1024]{2,1,0:T(8,128)(2,1)} async-done(((bf16[1,256,1024]{2,1,0:T(8,128)(2,1)}), bf16[1,1024,1024]{2,1,0:T(8,128)(2,1)}) %all-gather.11.cloned.1.call-update) | async-done | bytes 2097168 | tf_op jit(solution)/shard_map/all_gather | solution.py:42
  75.3 3.8 fusion.124
  81.3 23.8 %collective-permute-done = bf16[1,1024,1024]{2,1,0:T(8,128)(2,1)S(1)} collective-permute-done((bf16[1,1024,1024]{2,1,0:T(8,128)(2,1)}, bf16[1,1024,1024]{2,1,0:T(8,128)(2,1)S(1)}, u32[]{:S(2)}, u32[]{:S(2)}) %collective-permute-start) | collective-permute-done | bytes 2097184 | tf_op jit(solution)/shard_map/ppermute | solution.py:14
  106.7 3.5 all-gather.21.cloned.1.call-done
  112.6 30.6 %all-gather.13.cloned.1.call-done = bf16[1,1024,1024]{2,1,0:T(8,128)(2,1)} async-done(((bf16[1,256,1024]{2,1,0:T(8,128)(2,1)}), bf16[1,1024,1024]{2,1,0:T(8,128)(2,1)}) %all-gather.13.cloned.1.call-update) | async-done | bytes 2097168 | tf_op jit(solution)/shard_map/all_gather | solution.py:69
  143.2 16.6 %collective-permute-done.10 = bf16[1,1024,1024]{2,1,0:T(8,128)(2,1)} collective-permute-done((bf16[1,1024,1024]{2,1,0:T(8,128)(2,1)}, bf16[1,1024,1024]{2,1,0:T(8,128)(2,1)}, u32[]{:S(2)}, u32[]{:S(2)}) %collective-permute-start.10) | collective-permute-done | bytes 2097184 | tf_op jit(solution)/shard_map/ppermute | solution.py:14
  159.8 4.4 fusion.121
  164.3 2.5 collective-permute-start.1
  166.8 48.9 %collective-permute-done.1 = bf16[1,1024,1024]{2,1,0:T(8,128)(2,1)S(1)} collective-permute-done((bf16[1,1024,1024]{2,1,0:T(8,128)(2,1)}, bf16[1,1024,1024]{2,1,0:T(8,128)(2,1)S(1)}, u32[]{:S(2)}, u32[]{:S(2)}) %collective-permute-start.1) | collective-permute-done | bytes 2097184 | tf_op jit(solution)/shard_map/ppermute | solution.py:14
  217.4 3.3 collective-permute-start.11
  220.7 29.9 %all-gather.15.cloned.1.call-done = bf16[1,1024,1024]{2,1,0:T(8,128)(2,1)} async-done(((bf16[1,256,1024]{2,1,0:T(8,128)(2,1)}), bf16[1,1024,1024]{2,1,0:T(8,128)(2,1)}) %all-gather.15.cloned.1.call-update) | async-done | bytes 2097168 | tf_op jit(solution)/shard_map/all_gather | solution.py:69
  250.6 17.9 %collective-permute-done.11 = bf16[1,1024,1024]{2,1,0:T(8,128)(2,1)} collective-permute-done((bf16[1,1024,1024]{2,1,0:T(8,128)(2,1)}, bf16[1,1024,1024]{2,1,0:T(8,128)(2,1)}, u32[]{:S(2)}, u32[]{:S(2)}) %collective-permute-start.11) | collective-permute-done | bytes 2097184 | tf_op jit(solution)/shard_map/ppermute | solution.py:14
  268.5 4.4 fusion.118
  275.2 48.0 %collective-permute-done.2 = bf16[1,1024,1024]{2,1,0:T(8,128)(2,1)S(1)} collective-permute-done((bf16[1,1024,1024]{2,1,0:T(8,128)(2,1)}, bf16[1,1024,1024]{2,1,0:T(8,128)(2,1)S(1)}, u32[]{:S(2)}, u32[]{:S(2)}) %collective-permute-start.2) | collective-permute-done | bytes 2097184 | tf_op jit(solution)/shard_map/ppermute | solution.py:14
  324.8 2.5 collective-permute-start.12
  327.3 30.0 %all-gather.17.cloned.1.call-done = bf16[1,1024,1024]{2,1,0:T(8,128)(2,1)} async-done(((bf16[1,256,1024]{2,1,0:T(8,128)(2,1)}), bf16[1,1024,1024]{2,1,0:T(8,128)(2,1)}) %all-gather.17.cloned.1.call-update) | async-done | bytes 2097168 | tf_op jit(solution)/shard_map/all_gather | solution.py:69
  357.3 14.4 %collective-permute-done.12 = bf16[1,1024,1024]{2,1,0:T(8,128)(2,1)} collective-permute-done((bf16[1,1024,1024]{2,1,0:T(8,128)(2,1)}, bf16[1,1024,1024]{2,1,0:T(8,128)(2,1)}, u32[]{:S(2)}, u32[]{:S(2)}) %collective-permute-start.12) | collective-permute-done | bytes 2097184 | tf_op jit(solution)/shard_map/ppermute | solution.py:14
  371.7 4.4 fusion.115
  376.2 2.5 collective-permute-start.3
  378.7 7.8 %all_gather.49 = bf16[1,1024]{1,0:T(2,128)(2,1)S(1)} all-gather(bf16[1,256]{1,0:T(2,128)(2,1)S(1)} %copy-done.10), channel_id=1, replica_groups=mesh['tm'=32,'row'=4] {'row'}, dimensions={1}, use_global_device_ids=true | all-gather | bytes 2560 | tf_op jit(solution)/shard_map/all_gather | solution.py:43
  389.9 32.1 %collective-permute-done.3 = bf16[1,1024,1024]{2,1,0:T(8,128)(2,1)S(1)} collective-permute-done((bf16[1,1024,1024]{2,1,0:T(8,128)(2,1)}, bf16[1,1024,1024]{2,1,0:T(8,128)(2,1)S(1)}, u32[]{:S(2)}, u32[]{:S(2)}) %collective-permute-start.3) | collective-permute-done | bytes 2097184 | tf_op jit(solution)/shard_map/ppermute | solution.py:14
  423.6 7.9 %all_gather.50 = bf16[1,1024]{1,0:T(2,128)(2,1)S(1)} all-gather(bf16[1,256]{1,0:T(2,128)(2,1)S(1)} %get-tuple-element.9), channel_id=1, replica_groups=mesh['tm'=32,'row'=4] {'row'}, dimensions={1}, use_global_device_ids=true | all-gather | bytes 2560 | tf_op jit(solution)/shard_map/all_gather | solution.py:69
  433.9 3.7 collective-permute-done.5
  439.1 8.2 %all_gather.51 = bf16[1,1024]{1,0:T(2,128)(2,1)S(1)} all-gather(bf16[1,256]{1,0:T(2,128)(2,1)S(1)} %get-tuple-element.7), channel_id=1, replica_groups=mesh['tm'=32,'row'=4] {'row'}, dimensions={1}, use_global_device_ids=true | all-gather | bytes 2560 | tf_op jit(solution)/shard_map/all_gather | solution.py:69
  447.3 3.7 collective-permute-start.6
  451.0 34.6 %collective-permute-done.6 = bf16[1,1024]{1,0:T(2,128)(2,1)S(1)} collective-permute-done((bf16[1,1024]{1,0:T(2,128)(2,1)S(1)}, bf16[1,1024]{1,0:T(2,128)(2,1)S(1)}, u32[]{:S(2)}, u32[]{:S(2)}) %collective-permute-start.6) | collective-permute-done | bytes 2080 | tf_op jit(solution)/shard_map/ppermute | solution.py:14
  485.8 7.0 %all_gather.52 = bf16[1,1024]{1,0:T(2,128)(2,1)S(1)} all-gather(bf16[1,256]{1,0:T(2,128)(2,1)S(1)} %get-tuple-element.5), channel_id=1, replica_groups=mesh['tm'=32,'row'=4] {'row'}, dimensions={1}, use_global_device_ids=true | all-gather | bytes 2560 | tf_op jit(solution)/shard_map/all_gather | solution.py:69
  494.7 3.6 collective-permute-done.7
  498.6 9.0 %all_gather.53 = bf16[1,1024]{1,0:T(2,128)(2,1)S(1)} all-gather(bf16[1,256]{1,0:T(2,128)(2,1)S(1)} %get-tuple-element.3), channel_id=1, replica_groups=mesh['tm'=32,'row'=4] {'row'}, dimensions={1}, use_global_device_ids=true | all-gather | bytes 2560 | tf_op jit(solution)/shard_map/all_gather | solution.py:69
  508.8 5.7 %collective-permute-done.8 = bf16[1,1024]{1,0:T(2,128)(2,1)S(1)} collective-permute-done((bf16[1,1024]{1,0:T(2,128)(2,1)S(1)}, bf16[1,1024]{1,0:T(2,128)(2,1)S(1)}, u32[]{:S(2)}, u32[]{:S(2)}) %collective-permute-start.8) | collective-permute-done | bytes 2080 | tf_op jit(solution)/shard_map/ppermute | solution.py:14
  515.4 4.3 fusion.112
  (79 shorter events, 29.7 us)
Async XLA Ops:
  7.2 35.0 %all-gather.19.cloned.1.call-start = ((), (), s32[]{:S(2)}) async-start(), calls=%async_computation.4 | async-start | bytes 2621440 | tf_op jit(solution)/shard_map/all_gather | solution.py:44
  7.9 67.4 %all-gather.11.cloned.1.call-start = ((), (), s32[]{:S(2)}) async-start(), calls=%async_computation | async-start | bytes 2621440 | tf_op jit(solution)/shard_map/all_gather | solution.py:42
  9.9 100.3 %all-gather.21.cloned.1.call-start = ((), (), s32[]{:S(2)}) async-start(), calls=%async_computation.5 | async-start | bytes 2621440 | tf_op jit(solution)/shard_map/all_gather | solution.py:69
  42.2 33.1 %collective-permute-start.9 = (bf16[1,1024,1024]{2,1,0:T(8,128)(2,1)}, bf16[1,1024,1024]{2,1,0:T(8,128)(2,1)S(1)}, u32[]{:S(2)}, u32[]{:S(2)}) collective-permute-start(bf16[1,1024,1024]{2,1,0:T(8,128)(2,1)} %all-gather.19.cloned.1.call-done), channel_id=1, source_target_pairs={{4,0},{8,4},{12,8},{16,12},{20,16},{24,20},{28,24},{32,28},{36,32}... | collective-permute-start | bytes 6291464 | tf_op jit(solution)/shard_map/ppermute | solution.py:14
  79.2 80.6 %copy-start.9 = (bf16[1,256,1024]{2,1,0:T(8,128)(2,1)S(1)}, bf16[1,256,1024]{2,1,0:T(8,128)(2,1)}, u32[]{:S(2)}) copy-start(bf16[1,256,1024]{2,1,0:T(8,128)(2,1)} %fusion.124) | copy-start | bytes 1572868
  79.2 64.0 %all-gather.13.cloned.1.call-start = ((), (), s32[]{:S(2)}) async-start(), calls=%async_computation.1 | async-start | bytes 2621440 | tf_op jit(solution)/shard_map/all_gather | solution.py:69
  79.2 25.9 %collective-permute-start = (bf16[1,1024,1024]{2,1,0:T(8,128)(2,1)}, bf16[1,1024,1024]{2,1,0:T(8,128)(2,1)S(1)}, u32[]{:S(2)}, u32[]{:S(2)}) collective-permute-start(bf16[1,1024,1024]{2,1,0:T(8,128)(2,1)} %all-gather.11.cloned.1.call-done), channel_id=1, source_target_pairs={{4,0},{8,4},{12,8},{16,12},{20,16},{24,20},{28,24},{32,28},{36,32}... | collective-permute-start | bytes 6291464 | tf_op jit(solution)/shard_map/ppermute | solution.py:14
  106.7 110.7 %all-gather.23.cloned.1.call-start = ((), (), s32[]{:S(2)}) async-start(), calls=%async_computation.6 | async-start | bytes 2621440 | tf_op jit(solution)/shard_map/all_gather | solution.py:69
  110.2 49.6 %collective-permute-start.10 = (bf16[1,1024,1024]{2,1,0:T(8,128)(2,1)}, bf16[1,1024,1024]{2,1,0:T(8,128)(2,1)}, u32[]{:S(2)}, u32[]{:S(2)}) collective-permute-start(bf16[1,1024,1024]{2,1,0:T(8,128)(2,1)} %all-gather.21.cloned.1.call-done), channel_id=1, source_target_pairs={{8,0},{12,4},{16,8},{20,12},{24,16},{28,20},{32,24},{36,28},{40,32... | collective-permute-start | bytes 6291464 | tf_op jit(solution)/shard_map/ppermute | solution.py:14
  112.6 103.2 %copy-start.1 = (bf16[1,256,1024]{2,1,0:T(8,128)(2,1)S(1)}, bf16[1,256,1024]{2,1,0:T(8,128)(2,1)}, u32[]{:S(2)}) copy-start(bf16[1,256,1024]{2,1,0:T(8,128)(2,1)} %fusion.127) | copy-start | bytes 1572868
  164.3 104.2 %copy-start.7 = (bf16[1,256,1024]{2,1,0:T(8,128)(2,1)S(1)}, bf16[1,256,1024]{2,1,0:T(8,128)(2,1)}, u32[]{:S(2)}) copy-start(bf16[1,256,1024]{2,1,0:T(8,128)(2,1)} %fusion.121) | copy-start | bytes 1572868
  164.3 86.3 %all-gather.15.cloned.1.call-start = ((), (), s32[]{:S(2)}) async-start(), calls=%async_computation.2 | async-start | bytes 2621440 | tf_op jit(solution)/shard_map/all_gather | solution.py:69
  164.3 51.4 %collective-permute-start.1 = (bf16[1,1024,1024]{2,1,0:T(8,128)(2,1)}, bf16[1,1024,1024]{2,1,0:T(8,128)(2,1)S(1)}, u32[]{:S(2)}, u32[]{:S(2)}) collective-permute-start(bf16[1,1024,1024]{2,1,0:T(8,128)(2,1)} %all-gather.13.cloned.1.call-done), channel_id=1, source_target_pairs={{8,0},{12,4},{16,8},{20,12},{24,16},{28,20},{32,24},{36,28},{40,32... | collective-permute-start | bytes 6291464 | tf_op jit(solution)/shard_map/ppermute | solution.py:14
  217.3 107.5 %all-gather.25.cloned.1.call-start = ((), (), s32[]{:S(2)}) async-start(), calls=%async_computation.7 | async-start | bytes 2621440 | tf_op jit(solution)/shard_map/all_gather | solution.py:69
  217.4 51.1 %collective-permute-start.11 = (bf16[1,1024,1024]{2,1,0:T(8,128)(2,1)}, bf16[1,1024,1024]{2,1,0:T(8,128)(2,1)}, u32[]{:S(2)}, u32[]{:S(2)}) collective-permute-start(bf16[1,1024,1024]{2,1,0:T(8,128)(2,1)} %all-gather.23.cloned.1.call-done), channel_id=1, source_target_pairs={{16,0},{20,4},{24,8},{28,12},{32,16},{36,20},{40,24},{44,28},{48,3... | collective-permute-start | bytes 6291464 | tf_op jit(solution)/shard_map/ppermute | solution.py:14
  220.7 102.5 %copy-start.2 = (bf16[1,256,1024]{2,1,0:T(8,128)(2,1)S(1)}, bf16[1,256,1024]{2,1,0:T(8,128)(2,1)}, u32[]{:S(2)}) copy-start(bf16[1,256,1024]{2,1,0:T(8,128)(2,1)} %fusion.130) | copy-start | bytes 1572868
  272.9 98.7 %copy-start.8 = (bf16[1,256,1024]{2,1,0:T(8,128)(2,1)S(1)}, bf16[1,256,1024]{2,1,0:T(8,128)(2,1)}, u32[]{:S(2)}) copy-start(bf16[1,256,1024]{2,1,0:T(8,128)(2,1)} %fusion.118) | copy-start | bytes 1572868
  272.9 84.3 %all-gather.17.cloned.1.call-start = ((), (), s32[]{:S(2)}) async-start(), calls=%async_computation.3 | async-start | bytes 2621440 | tf_op jit(solution)/shard_map/all_gather | solution.py:69
  273.0 50.2 %collective-permute-start.2 = (bf16[1,1024,1024]{2,1,0:T(8,128)(2,1)}, bf16[1,1024,1024]{2,1,0:T(8,128)(2,1)S(1)}, u32[]{:S(2)}, u32[]{:S(2)}) collective-permute-start(bf16[1,1024,1024]{2,1,0:T(8,128)(2,1)} %all-gather.15.cloned.1.call-done), channel_id=1, source_target_pairs={{16,0},{20,4},{24,8},{28,12},{32,16},{36,20},{40,24},{44,28},{48,3... | collective-permute-start | bytes 6291464 | tf_op jit(solution)/shard_map/ppermute | solution.py:14
  324.7 113.1 %all-gather.27.cloned.1.call-start = ((), (), s32[]{:S(2)}) async-start(), calls=%async_computation.8 | async-start | bytes 2621440 | tf_op jit(solution)/shard_map/all_gather | solution.py:69
  324.8 46.9 %collective-permute-start.12 = (bf16[1,1024,1024]{2,1,0:T(8,128)(2,1)}, bf16[1,1024,1024]{2,1,0:T(8,128)(2,1)}, u32[]{:S(2)}, u32[]{:S(2)}) collective-permute-start(bf16[1,1024,1024]{2,1,0:T(8,128)(2,1)} %all-gather.25.cloned.1.call-done), channel_id=1, source_target_pairs={{32,0},{36,4},{40,8},{44,12},{48,16},{52,20},{56,24},{60,28},{64,3... | collective-permute-start | bytes 6291464 | tf_op jit(solution)/shard_map/ppermute | solution.py:14
  327.3 94.7 %copy-start.3 = (bf16[1,256,1024]{2,1,0:T(8,128)(2,1)S(1)}, bf16[1,256,1024]{2,1,0:T(8,128)(2,1)}, u32[]{:S(2)}) copy-start(bf16[1,256,1024]{2,1,0:T(8,128)(2,1)} %fusion.133) | copy-start | bytes 1572868
  376.1 139.2 %all-gather.29.cloned.1.call-start = ((), (), s32[]{:S(2)}) async-start(), calls=%async_computation.9 | async-start | bytes 2621440 | tf_op jit(solution)/shard_map/all_gather | solution.py:69
  376.2 45.8 %collective-permute-start.3 = (bf16[1,1024,1024]{2,1,0:T(8,128)(2,1)}, bf16[1,1024,1024]{2,1,0:T(8,128)(2,1)S(1)}, u32[]{:S(2)}, u32[]{:S(2)}) collective-permute-start(bf16[1,1024,1024]{2,1,0:T(8,128)(2,1)} %all-gather.17.cloned.1.call-done), channel_id=1, source_target_pairs={{32,0},{36,4},{40,8},{44,12},{48,16},{52,20},{56,24},{60,28},{64,3... | collective-permute-start | bytes 6291464 | tf_op jit(solution)/shard_map/ppermute | solution.py:14
  386.5 3.2 collective-permute-start.4
  423.5 91.0 %copy-start.4 = (bf16[1,256,1024]{2,1,0:T(8,128)(2,1)S(1)}, bf16[1,256,1024]{2,1,0:T(8,128)(2,1)}, u32[]{:S(2)}) copy-start(bf16[1,256,1024]{2,1,0:T(8,128)(2,1)} %fusion.136) | copy-start | bytes 1572868
  423.5 91.9 %copy-start.6 = (bf16[1,256,1024]{2,1,0:T(8,128)(2,1)S(1)}, bf16[1,256,1024]{2,1,0:T(8,128)(2,1)}, u32[]{:S(2)}) copy-start(bf16[1,256,1024]{2,1,0:T(8,128)(2,1)} %fusion.115) | copy-start | bytes 1572868
  431.5 6.0 %collective-permute-start.5 = (bf16[1,1024]{1,0:T(2,128)(2,1)S(1)}, bf16[1,1024]{1,0:T(2,128)(2,1)S(1)}, u32[]{:S(2)}, u32[]{:S(2)}) collective-permute-start(bf16[1,1024]{1,0:T(2,128)(2,1)S(1)} %all_gather.50), channel_id=1, source_target_pairs={{8,0},{12,4},{16,8},{20,12},{24,16},{28,20},{32,24},{36,28},{40,32... | collective-permute-start | bytes 6152 | tf_op jit(solution)/shard_map/ppermute | solution.py:14
  437.8 77.6 %collective-permute-start.13 = (bf16[1,1024,1024]{2,1,0:T(8,128)(2,1)}, bf16[1,1024,1024]{2,1,0:T(8,128)(2,1)}, u32[]{:S(2)}, u32[]{:S(2)}) collective-permute-start(bf16[1,1024,1024]{2,1,0:T(8,128)(2,1)} %all-gather.27.cloned.1.call-done), channel_id=1, source_target_pairs={{64,0},{68,4},{72,8},{76,12},{80,16},{84,20},{88,24},{92,28},{96,3... | collective-permute-start | bytes 6291464 | tf_op jit(solution)/shard_map/ppermute | solution.py:14
  447.3 38.3 %collective-permute-start.6 = (bf16[1,1024]{1,0:T(2,128)(2,1)S(1)}, bf16[1,1024]{1,0:T(2,128)(2,1)S(1)}, u32[]{:S(2)}, u32[]{:S(2)}) collective-permute-start(bf16[1,1024]{1,0:T(2,128)(2,1)S(1)} %all_gather.51), channel_id=1, source_target_pairs={{16,0},{20,4},{24,8},{28,12},{32,16},{36,20},{40,24},{44,28},{48,3... | collective-permute-start | bytes 6152 | tf_op jit(solution)/shard_map/ppermute | solution.py:14
  492.8 5.5 %collective-permute-start.7 = (bf16[1,1024]{1,0:T(2,128)(2,1)S(1)}, bf16[1,1024]{1,0:T(2,128)(2,1)S(1)}, u32[]{:S(2)}, u32[]{:S(2)}) collective-permute-start(bf16[1,1024]{1,0:T(2,128)(2,1)S(1)} %all_gather.52), channel_id=1, source_target_pairs={{32,0},{36,4},{40,8},{44,12},{48,16},{52,20},{56,24},{60,28},{64,3... | collective-permute-start | bytes 6152 | tf_op jit(solution)/shard_map/ppermute | solution.py:14
  507.6 7.0 %collective-permute-start.8 = (bf16[1,1024]{1,0:T(2,128)(2,1)S(1)}, bf16[1,1024]{1,0:T(2,128)(2,1)S(1)}, u32[]{:S(2)}, u32[]{:S(2)}) collective-permute-start(bf16[1,1024]{1,0:T(2,128)(2,1)S(1)} %all_gather.53), channel_id=1, source_target_pairs={{64,0},{68,4},{72,8},{76,12},{80,16},{84,20},{88,24},{92,28},{96,3... | collective-permute-start | bytes 6152 | tf_op jit(solution)/shard_map/ppermute | solution.py:14
  (3 other events, 180.6 us)
Sparse Core Ops, SparseCore 0:
  9.7 32.4 all-gather.18
  44.4 30.8 all-gather.10
  79.3 30.8 all-gather.20
  112.3 30.8 all-gather.12
  164.4 33.1 all-gather.22
  217.4 33.1 all-gather.14
  273.1 32.7 all-gather.24
  324.9 32.3 all-gather.16
  376.3 31.9 all-gather.26
  423.7 31.6 all-gather.28
where the time goes:
time: 527 us
  waiting for transfers between devices  409 us (78%)
  blocking collectives  39.9 us (8%)
  starting transfers between devices  32.1 us (6%)
  matrix products  28.6 us (5%)
  between operations  14.5 us (3%)
    ppermute x14, waiting for transfers between devices, passed_along(): return lax.ppermute(block, axis, route)  251 us
    all_gather x8, waiting for transfers between devices, per_device(): lax.all_gather(for_sending(own_part), 'row', axis=1, tiled=True)  93.9 us
    all_gather x1, waiting for transfers between devices, per_device(): lax.all_gather(own_part[2], 'row', axis=1, tiled=True)  32.3 us
    all_gather x4, blocking collectives, per_device(): lax.all_gather(for_sending(own_part), 'row', axis=1, tiled=True)  32.1 us
    ppermute x14, starting transfers between devices, passed_along(): return lax.ppermute(block, axis, route)  31.7 us
    all_gather x1, waiting for transfers between devices, per_device(): lax.all_gather(own_part[0], 'row', axis=1, tiled=True)  31.2 us
    dot_general x5, matrix products, compose(): lax.dot_general(middle, gain_whole[0], (((1,), (1,)), ((), ())), preferre...  21.4 us
  transfers between devices with their start and end apart: 24, of which 18 were waited for; matrix products, arithmetic and copies ran while one was open for 2% of the time, Pallas kernels for 0%

commit v1 on v0

v1 whole, which is shorter than its diff:
```python
import functools

import jax
import jax.numpy as jnp
from jax import lax
from jax.experimental import pallas as pl
from jax.experimental.pallas import tpu as pltpu
from jax.sharding import PartitionSpec as P

MESH = pl.DeviceIdType.MESH
BF16 = jnp.bfloat16
F32 = jnp.float32
SLAB = 16


def dot(a, b):
    return jnp.dot(a, b, preferred_element_type=F32)


def dot_t(a, b):
    return lax.dot_general(a, b, (((1,), (1,)), ((), ())), preferred_element_type=F32)


def kernel(
    steps, levels, tile,
    e_in, g_in, l_in, o_g, o_l,
    e_first, e_later, far_e, far_lg, mid_out, mid_in, own_lg, acc_e,
    ring_s, ring_r, swap_s, swap_r, fe_s, fe_r, fl_s, fl_r, gg_s, gg_r, fg_s, fg_r,
):
    k = lax.axis_index("tm")
    r = lax.axis_index("row")
    right, opp, left = (lax.rem(r + o, 4) for o in (1, 2, 3))

    def at_row(row):
        return (k, row)

    def at_step(step):
        return (step, r)

    def copy(src, dst, ssem, rsem, dev):
        return pltpu.make_async_remote_copy(
            src_ref=src, dst_ref=dst, send_sem=ssem, recv_sem=rsem, device_id=dev, device_id_type=MESH
        )

    barrier = pltpu.get_barrier_semaphore()
    partners = [at_row(right), at_row(opp), at_row(left)]
    for s in range(levels):
        partners.append(at_step(lax.rem(k + 2**s, steps)))
        if 2 ** (s + 1) != steps:
            partners.append(at_step(lax.rem(k + steps - 2**s, steps)))
    for dev in partners:
        pl.semaphore_signal(barrier, inc=1, device_id=dev, device_id_type=MESH)

    def blocks(s):
        return e_first if s == 0 else e_later.at[s - 1]

    def gain(s, a, b):
        return e_first[a, b] if s == 0 else e_later[s - 1, b, a]

    def ring(s, way, slot, blk, h):
        ref = blocks(s).at[blk, pl.ds(2 * h, 2)]
        dev = at_row(right if way == 0 else left)
        return copy(ref, ref, ring_s.at[s, way, slot], ring_r.at[s, way, slot], dev)

    def ring_start(s):
        ring(s, 0, 0, r, 0).start()
        ring(s, 1, 1, r, 1).start()
        ring(s, 0, 1, r, 1).start()
        ring(s, 1, 0, r, 0).start()

    def ring_relay(s):
        ring(s, 0, 0, left, 0).wait_recv()
        ring(s, 0, 2, left, 0).start()
        ring(s, 1, 1, right, 1).wait_recv()
        ring(s, 1, 2, right, 1).start()

    def ring_near(s):
        ring(s, 0, 1, left, 1).wait_recv()
        ring(s, 1, 0, right, 0).wait_recv()

    def ring_opp(s):
        ring(s, 0, 2, opp, 0).wait_recv()
        ring(s, 1, 2, opp, 1).wait_recv()

    def ring_sent(s):
        for way in range(2):
            ring(s, way, 0, r, 0).wait_send()
            ring(s, way, 1, r, 1).wait_send()
        ring(s, 0, 2, left, 0).wait_send()
        ring(s, 1, 2, right, 1).wait_send()

    def far_gain_piece(blk):
        return copy(e_first.at[blk, r], far_e.at[0, blk], fe_s.at[0, blk], fe_r.at[0, blk], at_step(k - 1))

    def far_gain(s):
        return copy(e_later.at[s - 1, r], far_e.at[s], fe_s.at[s, 0], fe_r.at[s, 0], at_step(k - 2**s))

    def far_spread(s):
        if s == 0:
            part = own_lg.at[:, pl.ds(0, tile), :]
            there = far_lg.at[0, :, pl.ds(0, tile), :]
        else:
            part = own_lg
            there = far_lg.at[s]
        return copy(part, there, fl_s.at[s], fl_r.at[s], at_step(k - 2**s))

    def far_offset():
        return copy(
            own_lg.at[:, pl.ds(tile, SLAB), :], far_lg.at[0, :, pl.ds(tile, SLAB), :], fg_s, fg_r, at_step(k - 1)
        )

    def offset_piece(o):
        ref = own_lg.at[r, pl.ds(tile, SLAB), :]
        return copy(ref, ref, gg_s.at[o], gg_r.at[o], at_row(lax.rem(r + o, 4)))

    def offset_landed(o):
        ref = own_lg.at[lax.rem(r + 4 - o, 4), pl.ds(tile, SLAB), :]
        return copy(ref, ref, gg_s.at[o], gg_r.at[o], at_row(lax.rem(r + o, 4)))

    def swap(s, o):
        return copy(
            mid_out.at[s, o], mid_in.at[s, r, pl.ds(0, tile), :], swap_s.at[s, o], swap_r.at[s, o],
            at_row(lax.rem(r + o, 4)),
        )

    def swap_landed(s, o):
        return copy(
            mid_out.at[s, o], mid_in.at[s, lax.rem(r + 4 - o, 4), pl.ds(0, tile), :], swap_s.at[s, o],
            swap_r.at[s, o], at_row(lax.rem(r + o, 4)),
        )

    def composes(s):
        return k + 2**s < steps

    def makes_gain(s):
        return k + 2 ** (s + 1) < steps

    def sends_gain(s):
        return jnp.logical_and(k >= 2**s, k + 2**s < steps)

    def sends_spread(s):
        return k >= 2**s

    for n in range(4):
        cols = slice(n * tile, (n + 1) * tile)
        e_first[r, n] = e_in[0, :, cols]
    pl.semaphore_wait(barrier, len(partners))

    @pl.when(composes(0))
    def _():
        ring_start(0)

    @pl.when(sends_gain(0))
    def _():
        far_gain_piece(r).start()

    for n in range(4):
        cols = slice(n * tile, (n + 1) * tile)
        own_lg[n, pl.ds(0, tile), :] = l_in[0, :, cols]
    first_row = lax.broadcasted_iota(jnp.int32, (SLAB, tile), 0) == 0
    slab = jnp.broadcast_to(g_in[...].astype(F32), (SLAB, tile))
    own_lg[r, pl.ds(tile, SLAB), :] = jnp.where(first_row, slab, 0.0).astype(BF16)
    for o in (1, 2, 3):
        offset_piece(o).start()

    @pl.when(sends_spread(0))
    def _():
        far_spread(0).start()

    for o in (1, 2, 3):
        offset_landed(o).wait_recv()

    @pl.when(sends_spread(0))
    def _():
        far_offset().start()

    for s in range(levels):
        more = s + 1 < levels

        @pl.when(composes(s))
        def _():
            ring_relay(s)
            ring_near(s)
            if s == 0:

                @pl.when(sends_gain(0))
                def _():
                    far_gain_piece(left).start()
                    far_gain_piece(right).start()

                ring_opp(0)

                @pl.when(sends_gain(0))
                def _():
                    far_gain_piece(opp).start()

            elif more:

                @pl.when(makes_gain(s))
                def _():
                    far_gain(s).wait_recv()

                    @pl.loop(0, 4)
                    def _(a):
                        acc_e[a] = (
                            dot(gain(s, a, r), far_e[s, r])
                            + dot(gain(s, a, left), far_e[s, left])
                            + dot(gain(s, a, right), far_e[s, right])
                        )

                ring_opp(s)
            else:
                ring_opp(s)

            if more:

                @pl.when(makes_gain(s))
                def _():
                    if s == 0:
                        for b in range(4):
                            far_gain_piece(b).wait_recv()

                        @pl.loop(0, 4)
                        def _(a):
                            total = dot(gain(s, a, 0), far_e[s, 0])
                            for b in range(1, 4):
                                total += dot(gain(s, a, b), far_e[s, b])
                            e_later[s, r, a] = total.astype(BF16)
                    else:

                        @pl.loop(0, 4)
                        def _(a):
                            total = acc_e[a] + dot(gain(s, a, opp), far_e[s, opp])
                            e_later[s, r, a] = total.astype(BF16)

                    ring_start(s + 1)

                    @pl.when(sends_gain(s + 1))
                    def _():
                        far_gain(s + 1).start()

            far_spread(s).wait_recv()
            if s == 0:
                far_offset().wait_recv()
            for o in (2, 1, 3, 0):
                a = lax.rem(r + o, 4)
                total = dot_t(gain(s, a, 0), far_lg[s, 0, pl.ds(0, tile), :])
                for b in range(1, 4):
                    total += dot_t(gain(s, a, b), far_lg[s, b, pl.ds(0, tile), :])
                if o == 0:
                    mid_in[s, r, pl.ds(0, tile), :] = total.astype(BF16)
                else:
                    mid_out[s, o] = total.astype(BF16)
                    swap(s, o).start()
            for b in range(4):
                mid_in[s, b, pl.ds(tile, SLAB), :] = far_lg[s, b, pl.ds(tile, SLAB), :]
            for o in (1, 3, 2):
                swap_landed(s, o).wait_recv()

        @pl.when(sends_spread(s))
        def _():
            far_spread(s).wait_send()
            if s == 0:
                far_offset().wait_send()

        if s == 0:
            for o in (1, 2, 3):
                offset_piece(o).wait_send()

        @pl.when(composes(s))
        def _():
            @pl.loop(0, 4)
            def _(n):
                total = own_lg[n].astype(F32)
                for b in range(4):
                    total += dot_t(mid_in[s, b], gain(s, n, b))
                own_lg[n] = total.astype(BF16)

        if more:

            @pl.when(sends_spread(s + 1))
            def _():
                far_spread(s + 1).start()

    for n in range(4):
        cols = slice(n * tile, (n + 1) * tile)
        o_l[0, :, cols] = own_lg[n, pl.ds(0, tile), :]
    o_g[...] = own_lg[r, pl.ds(tile, SLAB), :][0:1]

    for s in range(levels):

        @pl.when(composes(s))
        def _():
            ring_sent(s)
            for o in (1, 2, 3):
                swap(s, o).wait_send()

        if s == 0:

            @pl.when(sends_gain(0))
            def _():
                for b in range(4):
                    far_gain_piece(b).wait_send()

        else:

            @pl.when(sends_gain(s))
            def _():
                far_gain(s).wait_send()


def per_device(gain_mats, offsets, spread_mats):
    steps = lax.axis_size("tm")
    levels = steps.bit_length() - 1
    tile = gain_mats.shape[1]
    dma = pltpu.SemaphoreType.DMA
    tall = tile + SLAB
    flops = levels * 3 * 2 * tile * (4 * tile) ** 2
    return pl.pallas_call(
        functools.partial(kernel, steps, levels, tile),
        name="scan",
        out_shape=(
            jax.ShapeDtypeStruct(offsets.shape, BF16),
            jax.ShapeDtypeStruct(spread_mats.shape, BF16),
        ),
        in_specs=[pl.BlockSpec(memory_space=pltpu.VMEM)] * 3,
        out_specs=[pl.BlockSpec(memory_space=pltpu.VMEM)] * 2,
        scratch_shapes=[
            pltpu.VMEM((4, 4, tile, tile), BF16),
            pltpu.VMEM((levels - 1, 4, 4, tile, tile), BF16),
            pltpu.VMEM((levels - 1, 4, tile, tile), BF16),
            pltpu.VMEM((levels, 4, tall, tile), BF16),
            pltpu.VMEM((levels, 4, tile, tile), BF16),
            pltpu.VMEM((levels, 4, tall, tile), BF16),
            pltpu.VMEM((4, tall, tile), BF16),
            pltpu.VMEM((4, tile, tile), F32),
            dma((levels, 2, 3)), dma((levels, 2, 3)),
            dma((levels, 4)), dma((levels, 4)),
            dma((levels, 4)), dma((levels, 4)),
            dma((levels,)), dma((levels,)),
            dma((4,)), dma((4,)),
            dma, dma,
        ],
        compiler_params=pltpu.CompilerParams(
            collective_id=0, has_side_effects=True, vmem_limit_bytes=48 * 2**20
        ),
        cost_estimate=pl.CostEstimate(flops=flops, bytes_accessed=3 * tile * 4 * tile * 2, transcendentals=0),
    )(gain_mats, offsets, spread_mats)


def solution(mesh):
    in_specs = (P("tm", "row", None), P("tm", "row"), P("tm", "row", None))
    out_specs = (P("tm", "row"), P("tm", "row", None))
    return jax.shard_map(per_device, mesh=mesh, in_specs=in_specs, out_specs=out_specs, check_vma=False)
```

time: 527 us -> 173 us (0.33)
  the two profiles are of different devices: /device:TPU:66 before, /device:TPU:8 now
where the time goes in v1:
time: 173 us; the launch traced here: 172 us
  Pallas kernels  168 us (97%)
  local copies, waits for them, and re-layouts  4.11 us (2%)
    pallas_call x1, Pallas kernels, per_device(): pl.pallas_call(functools.partial(kernel, steps, levels, tile), name='scan...  168 us
    unnamed x8, local copies, waits for them, and re-layouts  4.11 us

profile of v1, /device:TPU:8, one launch (start us, length us, event | category | flops | bytes accessed | tf_op | source)
XLA Modules:
  0.0 172.3 jit_solution(6329545429222067412)
XLA Ops:
  0.6 0.0 copy-start
  0.6 1.0 copy-done
  1.7 0.0 copy-start.1
  1.7 1.0 copy-done.1
  2.7 0.0 copy-start.2
  2.7 0.7 copy-done.2
  3.4 167.5 %scan.1 = (bf16[1,256]{1,0:T(2,128)(2,1)S(1)}, bf16[1,256,1024]{2,1,0:T(8,128)(2,1)S(1)}) custom-call(bf16[1,256,1024]{2,1,0:T(8,128)(2,1)S(1)} %copy-done, bf16[1,256]{1,0:T(2,128)(2,1)S(1)} %copy-done.2, bf16[1,256,1024]{2,1,0:T(8,128)(2,1)S(1)} %copy-done.1), custom_call_target="tpu_custom_call" | custom-call | flops 8053063680 | bytes 1572864 | tf_op jit(solution)/shard_map/scan/pallas_call | solution.py:319
  170.9 0.6 copy.7
  171.5 0.8 copy.8
Async XLA Ops:
  0.6 1.0 copy-start
  1.7 1.0 copy-start.1
  2.7 0.7 copy-start.2

commit v2 on v1

--- a/solution.py
+++ b/solution.py
@@ -24,7 +24,7 @@
 def kernel(
     steps, levels, tile,
     e_in, g_in, l_in, o_g, o_l,
-    e_first, e_later, far_e, far_lg, mid_out, mid_in, own_lg, acc_e,
+    e_first, e_later, far_e, far_lg, mid_out, mid_in, own_lg, acc_e, acc_m,
     ring_s, ring_r, swap_s, swap_r, fe_s, fe_r, fl_s, fl_r, gg_s, gg_r, fg_s, fg_r,
 ):
     k = lax.axis_index("tm")
@@ -95,14 +95,11 @@
     def far_gain(s):
         return copy(e_later.at[s - 1, r], far_e.at[s], fe_s.at[s, 0], fe_r.at[s, 0], at_step(k - 2**s))
 
-    def far_spread(s):
-        if s == 0:
-            part = own_lg.at[:, pl.ds(0, tile), :]
-            there = far_lg.at[0, :, pl.ds(0, tile), :]
-        else:
-            part = own_lg
-            there = far_lg.at[s]
-        return copy(part, there, fl_s.at[s], fl_r.at[s], at_step(k - 2**s))
+    def far_spread(s, n):
+        rows = pl.ds(0, tile if s == 0 else tile + SLAB)
+        return copy(
+            own_lg.at[n, rows, :], far_lg.at[s, n, rows, :], fl_s.at[s, n], fl_r.at[s, n], at_step(k - 2**s)
+        )
 
     def far_offset():
         return copy(
@@ -165,7 +162,8 @@
 
     @pl.when(sends_spread(0))
     def _():
-        far_spread(0).start()
+        for n in range(4):
+            far_spread(0, n).start()
 
     for o in (1, 2, 3):
         offset_landed(o).wait_recv()
@@ -179,7 +177,8 @@
 
         @pl.when(composes(s))
         def _():
-            ring_relay(s)
+            if s == 0:
+                ring_relay(s)
             ring_near(s)
             if s == 0:
 
@@ -200,8 +199,7 @@
                 def _():
                     far_gain(s).wait_recv()
 
-                    @pl.loop(0, 4)
-                    def _(a):
+                    for a in range(4):
                         acc_e[a] = (
                             dot(gain(s, a, r), far_e[s, r])
                             + dot(gain(s, a, left), far_e[s, left])
@@ -220,16 +218,14 @@
                         for b in range(4):
                             far_gain_piece(b).wait_recv()
 
-                        @pl.loop(0, 4)
-                        def _(a):
+                        for a in range(4):
                             total = dot(gain(s, a, 0), far_e[s, 0])
                             for b in range(1, 4):
                                 total += dot(gain(s, a, b), far_e[s, b])
                             e_later[s, r, a] = total.astype(BF16)
                     else:
 
-                        @pl.loop(0, 4)
-                        def _(a):
+                        for a in range(4):
                             total = acc_e[a] + dot(gain(s, a, opp), far_e[s, opp])
                             e_later[s, r, a] = total.astype(BF16)
 
@@ -239,14 +235,18 @@
                     def _():
                         far_gain(s + 1).start()
 
-            far_spread(s).wait_recv()
+            for b in range(4):
+                far_spread(s, b).wait_recv()
+                if b == 3:
+                    break
+                for o in range(4):
+                    total = dot_t(gain(s, lax.rem(r + o, 4), b), far_lg[s, b, pl.ds(0, tile), :])
+                    acc_m[o] = total if b == 0 else acc_m[o] + total
             if s == 0:
                 far_offset().wait_recv()
             for o in (2, 1, 3, 0):
                 a = lax.rem(r + o, 4)
-                total = dot_t(gain(s, a, 0), far_lg[s, 0, pl.ds(0, tile), :])
-                for b in range(1, 4):
-                    total += dot_t(gain(s, a, b), far_lg[s, b, pl.ds(0, tile), :])
+                total = acc_m[o] + dot_t(gain(s, a, 3), far_lg[s, 3, pl.ds(0, tile), :])
                 if o == 0:
                     mid_in[s, r, pl.ds(0, tile), :] = total.astype(BF16)
                 else:
@@ -254,12 +254,19 @@
                     swap(s, o).start()
             for b in range(4):
                 mid_in[s, b, pl.ds(tile, SLAB), :] = far_lg[s, b, pl.ds(tile, SLAB), :]
+            if more:
+
+                @pl.when(makes_gain(s))
+                def _():
+                    ring_relay(s + 1)
+
             for o in (1, 3, 2):
                 swap_landed(s, o).wait_recv()
 
         @pl.when(sends_spread(s))
         def _():
-            far_spread(s).wait_send()
+            for n in range(4):
+                far_spread(s, n).wait_send()
             if s == 0:
                 far_offset().wait_send()
 
@@ -269,18 +276,23 @@
 
         @pl.when(composes(s))
         def _():
-            @pl.loop(0, 4)
-            def _(n):
+            for n in range(4):
                 total = own_lg[n].astype(F32)
                 for b in range(4):
                     total += dot_t(mid_in[s, b], gain(s, n, b))
                 own_lg[n] = total.astype(BF16)
+                if more:
+
+                    @pl.when(sends_spread(s + 1))
+                    def _():
+                        far_spread(s + 1, n).start()
 
         if more:
 
-            @pl.when(sends_spread(s + 1))
+            @pl.when(jnp.logical_and(sends_spread(s + 1), jnp.logical_not(composes(s))))
             def _():
-                far_spread(s + 1).start()
+                for n in range(4):
+                    far_spread(s + 1, n).start()
 
     for n in range(4):
         cols = slice(n * tile, (n + 1) * tile)
@@ -334,10 +346,11 @@
             pltpu.VMEM((levels, 4, tall, tile), BF16),
             pltpu.VMEM((4, tall, tile), BF16),
             pltpu.VMEM((4, tile, tile), F32),
+            pltpu.VMEM((4, tile, tile), F32),
             dma((levels, 2, 3)), dma((levels, 2, 3)),
             dma((levels, 4)), dma((levels, 4)),
             dma((levels, 4)), dma((levels, 4)),
-            dma((levels,)), dma((levels,)),
+            dma((levels, 4)), dma((levels, 4)),
             dma((4,)), dma((4,)),
             dma, dma,
         ],

time: 173 us -> 151 us (0.87)
  the two profiles are of different devices: /device:TPU:8 before, /device:TPU:1 now
where the time goes in v2:
time: 151 us
  Pallas kernels  146 us (97%)
  local copies, waits for them, and re-layouts  4.11 us (3%)
    pallas_call x1, Pallas kernels, per_device(): pl.pallas_call(functools.partial(kernel, steps, levels, tile), name='scan...  146 us
    unnamed x8, local copies, waits for them, and re-layouts  4.11 us

profile of v2, /device:TPU:1, one launch (start us, length us, event | category | flops | bytes accessed | tf_op | source)
XLA Modules:
  0.0 151.2 jit_solution(12715474642900200527)
XLA Ops:
  0.6 0.0 copy-start
  0.6 1.0 copy-done
  1.7 0.0 copy-start.1
  1.7 1.0 copy-done.1
  2.7 0.0 copy-start.2
  2.7 0.7 copy-done.2
  3.4 146.4 %scan.1 = (bf16[1,256]{1,0:T(2,128)(2,1)S(1)}, bf16[1,256,1024]{2,1,0:T(8,128)(2,1)S(1)}) custom-call(bf16[1,256,1024]{2,1,0:T(8,128)(2,1)S(1)} %copy-done, bf16[1,256]{1,0:T(2,128)(2,1)S(1)} %copy-done.2, bf16[1,256,1024]{2,1,0:T(8,128)(2,1)S(1)} %copy-done.1), custom_call_target="tpu_custom_call" | custom-call | flops 8053063680 | bytes 1572864 | tf_op jit(solution)/shard_map/scan/pallas_call | solution.py:331
  149.8 0.6 copy.7
  150.4 0.8 copy.8
Async XLA Ops:
  0.6 1.0 copy-start
  1.7 1.0 copy-start.1
  2.7 0.7 copy-start.2

commit v3 on v0

v3 whole, which is shorter than its diff:
```python
import functools

import jax
import jax.numpy as jnp
from jax import lax
from jax.experimental import pallas as pl
from jax.experimental.pallas import tpu as pltpu
from jax.sharding import PartitionSpec as P

MESH = pl.DeviceIdType.MESH
BF16 = jnp.bfloat16
F32 = jnp.float32
SLAB = 16


def dot(a, b):
    return jnp.dot(a, b, preferred_element_type=F32)


def dot_t(a, b):
    return lax.dot_general(a, b, (((1,), (1,)), ((), ())), preferred_element_type=F32)


def kernel(
    steps, levels, tile,
    e_in, g_in, l_in, o_g, o_l,
    stage_e, stage_l, stage_g, e_first, e_later, far_e, far_l, far_g, own_l, own_g, mid, acc_e, fin_l, fin_g,
    mve_s, mve_r, mvl_s, mvl_r, fed_s, fed_r, fe_s, fe_r, gd_s, gd_r, fgd_s, fgd_r, fg_s, fg_r,
    sib_s, sib_r, par_s, par_r, fwd_s, fwd_r,
    lf_s, lf_r, ls_s, ls_r, lp_s, lp_r, lw_s, lw_r, fin_s, fin_r, fing_s, fing_r,
):
    k = lax.axis_index("tm")
    y = lax.axis_index("row")
    core = k % 2
    column = k // 2
    parity = y // 2
    e = 2 * column + parity
    first = y + parity * (3 - 2 * y)
    q = first + core * (3 - 2 * first)
    q_sib = 3 - q
    q_par = q + 1 - 2 * (q % 2)
    q_dia = 3 - q_par
    sib = (k + 1 - 2 * core, y)
    par = (k, y + 1 - 2 * (y % 2))
    stays = parity == core
    moves = parity != core
    partner = (k + 1 - 2 * core, 3 - y)

    def holder(element, quarter):
        c = quarter // 2
        b = quarter + c * (3 - 2 * quarter)
        p = element % 2
        return (2 * (element // 2) + c, b + p * (3 - 2 * b))

    def copy(src, dst, ssem, rsem, dev):
        return pltpu.make_async_remote_copy(
            src_ref=src, dst_ref=dst, send_sem=ssem, recv_sem=rsem, device_id=dev, device_id_type=MESH
        )

    def composes(el, s):
        return el + 2**s < steps

    def makes_gain(el, s):
        return el + 2 ** (s + 1) < steps

    def sends_gain(el, s):
        return jnp.logical_and(el >= 2**s, el + 2**s < steps)

    def both(a, b):
        return jnp.logical_and(a, b)

    feeds_self = both(core == 1, y < 2)

    barrier = pltpu.get_barrier_semaphore()

    def greet(dev):
        pl.semaphore_signal(barrier, inc=1, device_id=dev, device_id_type=MESH)

    greet(sib)
    greet(par)
    for row in range(4):

        @pl.when(jnp.logical_not(both(stays, row == y)))
        def _():
            greet((e, row))

        @pl.when(both(e + 1 < steps, jnp.logical_not(both(feeds_self, row == y))))
        def _():
            greet((e + 1, row))

    for s in range(1, levels):

        @pl.when(composes(e, s))
        def _():
            greet((k + 2**s, y))

    def count(flag):
        return flag.astype(jnp.int32)

    greetings = 2 + 4 - count(stays) + count(k >= 1) * (4 - count(feeds_self))
    for s in range(1, levels):
        greetings += count(e >= 2**s)

    def blocks(s):
        return e_first if s == 0 else e_later.at[s - 1]

    def gain(s, a, b):
        return e_first[a, b] if s == 0 else e_later[s - 1, b, a]

    def half(s, blk, h):
        return blocks(s).at[blk, pl.ds(2 * h, 2)]

    def gain_sib(s, h):
        return copy(half(s, q, h), half(s, q, h), sib_s.at[s, h], sib_r.at[s, h], sib)

    def gain_sib_in(s, h):
        return copy(half(s, q_sib, h), half(s, q_sib, h), sib_s.at[s, h], sib_r.at[s, h], sib)

    def gain_par(s, h):
        return copy(half(s, q, h), half(s, q, h), par_s.at[s, h], par_r.at[s, h], par)

    def gain_par_in(s, h):
        return copy(half(s, q_par, h), half(s, q_par, h), par_s.at[s, h], par_r.at[s, h], par)

    def gain_fwd(s, h):
        return copy(half(s, q_par, h), half(s, q_par, h), fwd_s.at[s, h], fwd_r.at[s, h], sib)

    def gain_fwd_in(s, h):
        return copy(half(s, q_dia, h), half(s, q_dia, h), fwd_s.at[s, h], fwd_r.at[s, h], sib)

    def gain_start(s, h):
        gain_par(s, h).start()
        gain_sib(s, h).start()

    def far_gain(s):
        return copy(e_later.at[s - 1, q], far_e.at[s], fe_s.at[s], fe_r.at[s], (k - 2**s, y))

    def far_offset(s):
        return copy(own_g, far_g.at[s], fg_s.at[s], fg_r.at[s], (k - 2**s, y))

    def far_tile(s, t):
        return copy(own_l.at[(q + t) % 4], far_l.at[s, 3 * q + t], lf_s.at[s, t], lf_r.at[s, t], (k - 2**s, y))

    def tile_copy(s, t, owner, ssem, rsem, dev):
        ref = far_l.at[s, 3 * owner + t]
        return copy(ref, ref, ssem.at[s, t], rsem.at[s, t], dev)

    def tile_sib(s, t):
        return tile_copy(s, t, q, ls_s, ls_r, sib)

    def tile_sib_in(s, t):
        return tile_copy(s, t, q_sib, ls_s, ls_r, sib)

    def tile_par(s, t):
        return tile_copy(s, t, q, lp_s, lp_r, par)

    def tile_par_in(s, t):
        return tile_copy(s, t, q_par, lp_s, lp_r, par)

    def tile_fwd(s, t):
        return tile_copy(s, t, q_par, lw_s, lw_r, sib)

    def tile_fwd_in(s, t):
        return tile_copy(s, t, q_dia, lw_s, lw_r, sib)

    def if_tile(t, whose, run):
        if t < 2:
            run()
        else:
            pl.when(whose == 0)(run)

    def spread(s, a, b):
        t = (b - a) % 4
        if t < 2 or (t == 2 and a < 2):
            return far_l[s, 3 * a + t], False
        return far_l[s, 3 * b + (4 - t)], True

    def move_gain(h):
        return copy(stage_e.at[pl.ds(2 * h, 2)], e_first.at[y, pl.ds(2 * h, 2)], mve_s.at[h], mve_r.at[h], partner)

    def move_gain_in(h):
        return copy(stage_e.at[pl.ds(2 * h, 2)], e_first.at[q, pl.ds(2 * h, 2)], mve_s.at[h], mve_r.at[h], partner)

    def move_spread():
        return copy(stage_l, own_l, mvl_s, mvl_r, partner)

    def gain_direct(quarter):
        return copy(
            stage_e.at[quarter], far_e.at[0, y], fed_s.at[quarter], fed_r.at[y], holder(k - 1, quarter)
        )

    def gain_direct_in(row):
        return copy(stage_e.at[0], far_e.at[0, row], fed_s.at[row], fed_r.at[row], sib)

    def tile_direct(t):
        return copy(
            stage_l.at[(y + t) % 4], far_l.at[0, 3 * y + t], lf_s.at[0, t], lf_r.at[0, t], holder(k - 1, y)
        )

    def tile_in(s, t):
        return copy(own_l.at[0], far_l.at[s, 3 * q + t], lf_s.at[s, t], lf_r.at[s, t], sib)

    def offset_direct(quarter):
        return copy(stage_g, own_g.at[y], gd_s.at[quarter], gd_r.at[y], holder(k, quarter))

    def offset_direct_in(row):
        return copy(stage_g, own_g.at[row], gd_s.at[row], gd_r.at[row], sib)

    def offset_direct_far(quarter):
        return copy(stage_g, far_g.at[0, y], fgd_s.at[quarter], fgd_r.at[y], holder(k - 1, quarter))

    def offset_direct_far_in(row):
        return copy(stage_g, far_g.at[0, row], fgd_s.at[row], fgd_r.at[row], sib)

    def back(n):
        return copy(own_l.at[n], fin_l.at[n], fin_s.at[n], fin_r.at[n], partner)

    def back_offset():
        return copy(own_g.at[q], fin_g, fing_s, fing_r, partner)

    input_gain_sent = both(k >= 1, makes_gain(k - 1, 0))

    for n in range(4):
        stage_e[n] = e_in[0, :, n * tile : (n + 1) * tile]

    @pl.when(stays)
    def _():
        for n in range(4):
            e_first[q, n] = e_in[0, :, n * tile : (n + 1) * tile]

    pl.semaphore_wait(barrier, greetings)

    @pl.when(both(moves, composes(k, 0)))
    def _():
        move_gain(0).start()
        move_gain(1).start()

    @pl.when(both(stays, composes(e, 0)))
    def _():
        gain_start(0, 0)
        gain_start(0, 1)

    @pl.when(input_gain_sent)
    def _():
        for quarter in range(4):
            here = both(feeds_self, quarter == 3 - y)

            @pl.when(jnp.logical_not(here))
            def _():
                gain_direct(quarter).start()

            @pl.when(here)
            def _():
                far_e[0, y] = stage_e[quarter]

    for n in range(4):
        stage_l[n] = l_in[0, :, n * tile : (n + 1) * tile]
    first_row = lax.broadcasted_iota(jnp.int32, (SLAB, tile), 0) == 0
    slab = jnp.broadcast_to(g_in[...].astype(F32), (SLAB, tile))
    stage_g[...] = jnp.where(first_row, slab, 0.0).astype(BF16)

    @pl.when(k >= 1)
    def _():
        for t in range(3):
            if_tile(t, y // 2, lambda t=t: tile_direct(t).start())

    @pl.when(moves)
    def _():
        move_spread().start()

    for quarter in range(4):
        here = both(stays, quarter == y)

        @pl.when(jnp.logical_not(here))
        def _():
            offset_direct(quarter).start()

        @pl.when(here)
        def _():
            own_g[y] = stage_g[...]

    @pl.when(k >= 1)
    def _():
        for quarter in range(4):
            here = both(feeds_self, quarter == 3 - y)

            @pl.when(jnp.logical_not(here))
            def _():
                offset_direct_far(quarter).start()

            @pl.when(here)
            def _():
                far_g[0, y] = stage_g[...]

    @pl.when(stays)
    def _():
        for n in range(4):
            own_l[n] = l_in[0, :, n * tile : (n + 1) * tile]

    @pl.when(both(moves, composes(e, 0)))
    def _():
        move_gain_in(0).wait_recv()
        gain_start(0, 0)
        move_gain_in(1).wait_recv()
        gain_start(0, 1)

    for s in range(levels):
        more = s + 1 < levels

        def tiles_out():
            for t in range(3):

                def run(t=t):
                    tile_in(s, t).wait_recv()
                    tile_par(s, t).start()
                    tile_sib(s, t).start()

                if_tile(t, core, run)

        def tiles_on():
            for t in range(3):

                def run(t=t):
                    tile_par_in(s, t).wait_recv()
                    tile_fwd(s, t).start()

                if_tile(t, core, run)

        def tiles_rest():
            for t in range(3):

                def run(t=t):
                    tile_sib_in(s, t).wait_recv()
                    tile_fwd_in(s, t).wait_recv()

                if_tile(t, 1 - core, run)

        def gain_on(h):
            gain_par_in(s, h).wait_recv()
            gain_fwd(s, h).start()

        @pl.when(composes(e, s))
        def _():
            gain_on(0)
            tiles_out()
            gain_on(1)
            for h in range(2):
                gain_sib_in(s, h).wait_recv()

            if more:

                @pl.when(makes_gain(e, s))
                def _():
                    if s == 0:
                        for row in range(4):

                            @pl.when(jnp.logical_not(both(feeds_self, row == y)))
                            def _():
                                gain_direct_in(row).wait_recv()

                    else:
                        copy(far_e.at[s], far_e.at[s], fe_s.at[s], fe_r.at[s], sib).wait_recv()
                        for a in range(4):
                            acc_e[a] = (
                                dot(gain(s, a, q), far_e[s, q])
                                + dot(gain(s, a, q_sib), far_e[s, q_sib])
                                + dot(gain(s, a, q_par), far_e[s, q_par])
                            )

            for h in range(2):
                gain_fwd_in(s, h).wait_recv()

            if more:

                @pl.when(makes_gain(e, s))
                def _():
                    for h in range(2):
                        for a in (2 * h, 2 * h + 1):
                            if s == 0:
                                total = dot(gain(s, a, 0), far_e[s, 0])
                                for b in range(1, 4):
                                    total += dot(gain(s, a, b), far_e[s, b])
                            else:
                                total = acc_e[a] + dot(gain(s, a, q_dia), far_e[s, q_dia])
                            e_later[s, q, a] = total.astype(BF16)
                        gain_start(s + 1, h)

                    @pl.when(sends_gain(e, s + 1))
                    def _():
                        far_gain(s + 1).start()

            tiles_on()
            tiles_rest()
            for n in range(4):
                total = None
                for b in range(4):
                    part, turned = spread(s, b, n)
                    term = (dot_t if turned else dot)(gain(s, q, b), part)
                    total = term if total is None else total + term
                mid[n, pl.ds(0, tile), :] = total.astype(BF16)
            if s == 0:
                for row in range(4):

                    @pl.when(jnp.logical_not(both(feeds_self, row == y)))
                    def _():
                        offset_direct_far_in(row).wait_recv()

            else:
                copy(far_g.at[s], far_g.at[s], fg_s.at[s], fg_r.at[s], sib).wait_recv()
            for b in range(4):
                mid[b, pl.ds(tile, SLAB), :] = far_g[s, b]

        if s == 0:

            @pl.when(moves)
            def _():
                move_spread().wait_recv()

            for row in range(4):

                @pl.when(jnp.logical_not(both(stays, row == y)))
                def _():
                    offset_direct_in(row).wait_recv()

        else:

            @pl.when(e >= 2**s)
            def _():
                for t in range(3):
                    if_tile(t, core, lambda t=t: far_tile(s, t).wait_send())
                far_offset(s).wait_send()

        @pl.when(composes(e, s))
        def _():
            for o in range(4):
                n = (q + o) % 4
                total = dot_t(mid[0], gain(s, n, 0))
                for b in range(1, 4):
                    total += dot_t(mid[b], gain(s, n, b))
                own_l[n] = (total[0:tile] + own_l[n].astype(F32)).astype(BF16)
                own_g[n] = (total[tile:] + own_g[n].astype(F32)).astype(BF16)
                if more:
                    if o < 3:

                        @pl.when(e >= 2 ** (s + 1))
                        def _():
                            if_tile(o, core, lambda: far_tile(s + 1, o).start())

                else:

                    @pl.when(moves)
                    def _():
                        back(n).start()

        if more:

            @pl.when(both(e >= 2 ** (s + 1), jnp.logical_not(composes(e, s))))
            def _():
                for t in range(3):
                    if_tile(t, core, lambda t=t: far_tile(s + 1, t).start())

            @pl.when(e >= 2 ** (s + 1))
            def _():
                far_offset(s + 1).start()

        else:

            @pl.when(both(moves, jnp.logical_not(composes(e, s))))
            def _():
                for n in range(4):
                    back(n).start()

    @pl.when(moves)
    def _():
        back_offset().start()
        for o in range(4):
            n = (y + o) % 4
            copy(own_l.at[n], fin_l.at[n], fin_s.at[n], fin_r.at[n], partner).wait_recv()
        for n in range(4):
            o_l[0, :, n * tile : (n + 1) * tile] = fin_l[n]
        back_offset().wait_recv()
        o_g[...] = fin_g[0:1]

    @pl.when(stays)
    def _():
        for n in range(4):
            o_l[0, :, n * tile : (n + 1) * tile] = own_l[n]
        o_g[...] = own_g[q][0:1]

    @pl.when(moves)
    def _():
        back_offset().wait_send()
        for n in range(4):
            back(n).wait_send()
        move_spread().wait_send()

    @pl.when(both(moves, composes(k, 0)))
    def _():
        move_gain(0).wait_send()
        move_gain(1).wait_send()

    for quarter in range(4):
        here = both(feeds_self, quarter == 3 - y)

        @pl.when(both(input_gain_sent, jnp.logical_not(here)))
        def _():
            gain_direct(quarter).wait_send()

        @pl.when(both(k >= 1, jnp.logical_not(here)))
        def _():
            offset_direct_far(quarter).wait_send()

        @pl.when(jnp.logical_not(both(stays, quarter == y)))
        def _():
            offset_direct(quarter).wait_send()

    @pl.when(k >= 1)
    def _():
        for t in range(3):
            if_tile(t, y // 2, lambda t=t: tile_direct(t).wait_send())

    for s in range(levels):

        @pl.when(composes(e, s))
        def _():
            for h in range(2):
                gain_par(s, h).wait_send()
                gain_sib(s, h).wait_send()
                gain_fwd(s, h).wait_send()
            for t in range(3):

                def run(t=t):
                    tile_par(s, t).wait_send()
                    tile_sib(s, t).wait_send()
                    tile_fwd(s, t).wait_send()

                if_tile(t, core, run)

        if s > 0:

            @pl.when(sends_gain(e, s))
            def _():
                far_gain(s).wait_send()


def per_device(gain_mats, offsets, spread_mats):
    steps = lax.axis_size("tm")
    levels = steps.bit_length() - 1
    tile = gain_mats.shape[1]
    dma = pltpu.SemaphoreType.DMA
    flops = levels * 3 * 2 * tile * (4 * tile) ** 2
    square = (tile, tile)
    return pl.pallas_call(
        functools.partial(kernel, steps, levels, tile),
        name="scan",
        out_shape=(
            jax.ShapeDtypeStruct(offsets.shape, BF16),
            jax.ShapeDtypeStruct(spread_mats.shape, BF16),
        ),
        in_specs=[pl.BlockSpec(memory_space=pltpu.VMEM)] * 3,
        out_specs=[pl.BlockSpec(memory_space=pltpu.VMEM)] * 2,
        scratch_shapes=[
            pltpu.VMEM((4, *square), BF16),
            pltpu.VMEM((4, *square), BF16),
            pltpu.VMEM((SLAB, tile), BF16),
            pltpu.VMEM((4, 4, *square), BF16),
            pltpu.VMEM((levels - 1, 4, 4, *square), BF16),
            pltpu.VMEM((levels - 1, 4, *square), BF16),
            pltpu.VMEM((levels, 12, *square), BF16),
            pltpu.VMEM((levels, 4, SLAB, tile), BF16),
            pltpu.VMEM((4, *square), BF16),
            pltpu.VMEM((4, SLAB, tile), BF16),
            pltpu.VMEM((4, tile + SLAB, tile), BF16),
            pltpu.VMEM((4, *square), F32),
            pltpu.VMEM((4, *square), BF16),
            pltpu.VMEM((SLAB, tile), BF16),
            dma((2,)), dma((2,)), dma, dma,
            dma((4,)), dma((4,)), dma((levels,)), dma((levels,)),
            dma((4,)), dma((4,)), dma((4,)), dma((4,)), dma((levels,)), dma((levels,)),
            dma((levels, 2)), dma((levels, 2)), dma((levels, 2)), dma((levels, 2)), dma((levels, 2)), dma((levels, 2)),
            dma((levels, 3)), dma((levels, 3)), dma((levels, 3)), dma((levels, 3)),
            dma((levels, 3)), dma((levels, 3)), dma((levels, 3)), dma((levels, 3)),
            dma((4,)), dma((4,)), dma, dma,
        ],
        compiler_params=pltpu.CompilerParams(
            collective_id=0, has_side_effects=True, vmem_limit_bytes=48 * 2**20
        ),
        cost_estimate=pl.CostEstimate(flops=flops, bytes_accessed=3 * tile * 4 * tile * 2, transcendentals=0),
    )(gain_mats, offsets, spread_mats)


def solution(mesh):
    in_specs = (P("tm", "row", None), P("tm", "row"), P("tm", "row", None))
    out_specs = (P("tm", "row"), P("tm", "row", None))
    return jax.shard_map(per_device, mesh=mesh, in_specs=in_specs, out_specs=out_specs, check_vma=False)
```

time: 527 us -> 147 us (0.28)
  the two profiles are of different devices: /device:TPU:66 before, /device:TPU:3 now
where the time goes in v3:
time: 147 us
  Pallas kernels  142 us (97%)
  local copies, waits for them, and re-layouts  4.11 us (3%)
    pallas_call x1, Pallas kernels, per_device(): pl.pallas_call(functools.partial(kernel, steps, levels, tile), name='scan...  142 us
    unnamed x8, local copies, waits for them, and re-layouts  4.11 us

profile of v3, /device:TPU:3, one launch (start us, length us, event | category | flops | bytes accessed | tf_op | source)
XLA Modules:
  0.0 146.6 jit_solution(8816549648843088498)
XLA Ops:
  0.6 0.0 copy-start
  0.6 1.0 copy-done
  1.7 0.0 copy-start.1
  1.7 1.0 copy-done.1
  2.7 0.0 copy-start.2
  2.7 0.7 copy-done.2
  3.4 141.9 %scan.1 = (bf16[1,256]{1,0:T(2,128)(2,1)S(1)}, bf16[1,256,1024]{2,1,0:T(8,128)(2,1)S(1)}) custom-call(bf16[1,256,1024]{2,1,0:T(8,128)(2,1)S(1)} %copy-done, bf16[1,256]{1,0:T(2,128)(2,1)S(1)} %copy-done.2, bf16[1,256,1024]{2,1,0:T(8,128)(2,1)S(1)} %copy-done.1), custom_call_target="tpu_custom_call" | custom-call | flops 8053063680 | bytes 1572864 | tf_op jit(solution)/shard_map/scan/pallas_call | solution.py:553
  145.3 0.6 copy.7
  145.8 0.8 copy.8
Async XLA Ops:
  0.6 1.0 copy-start
  1.7 1.0 copy-start.1
  2.7 0.7 copy-start.2

commit v4 on v3

v4 whole, which is shorter than its diff:
```python
import functools

import jax
import jax.numpy as jnp
from jax import lax
from jax.experimental import pallas as pl
from jax.experimental.pallas import tpu as pltpu
from jax.sharding import PartitionSpec as P

MESH = pl.DeviceIdType.MESH
BF16 = jnp.bfloat16
F32 = jnp.float32
PLAN = (
    "D0", "T0", "P0", "O0", "B00", "B01", "g00", "t00", "t01", "g01", "b0", "n0", "w0", "E0", "F10", "F11", "F12", "F13", "H1", "t02",
    "t03", "t04", "t05", "G10", "G11", "u00", "u01", "u02", "u03", "u04", "u05", "M0", "L0", "g10", "t10", "t11", "g11", "b1", "n1", "w1",
    "E1", "F20", "F21", "F22", "F23", "H2", "t12", "t13", "t14", "t15", "G20", "G21", "u10", "u11", "u12", "u13", "u14", "u15", "M1", "L1",
    "g20", "t20", "t21", "g21", "b2", "n2", "w2", "E2", "F30", "F31", "F32", "F33", "H3", "t22", "t23", "t24", "t25", "G30", "G31", "u20",
    "u21", "u22", "u23", "u24", "u25", "M2", "L2", "g30", "t30", "t31", "g31", "b3", "n3", "w3", "E3", "F40", "F41", "F42", "F43", "H4",
    "t32", "t33", "t34", "t35", "G40", "G41", "u30", "u31", "u32", "u33", "u34", "u35", "M3", "L3", "g40", "t40", "t41", "g41", "b4", "w4",
    "t42", "t43", "t44", "t45", "u40", "u41", "u42", "u43", "u44", "u45", "M4", "L4",
)
HALVES = 2
FARS = 4
PARTS = 2
SLAB = 16


def dot(a, b):
    return jnp.dot(a, b, preferred_element_type=F32)


def dot_t(a, b):
    return lax.dot_general(a, b, (((1,), (1,)), ((), ())), preferred_element_type=F32)


def kernel(
    steps, levels, tile,
    e_in, g_in, l_in, o_g, o_l,
    stage_e, stage_l, stage_g, e_first, e_later, far_e, far_l, far_g, own_l, own_g, mid, acc_e, fin_l, fin_g, offset_row,
    mve_s, mve_r, mvl_s, mvl_r, fed_s, fed_r, fe_s, fe_r, gd_s, gd_r, fgd_s, fgd_r, fg_s, fg_r,
    sib_s, sib_r, par_s, par_r, fwd_s, fwd_r,
    lf_s, lf_r, ls_s, ls_r, lp_s, lp_r, lw_s, lw_r, fin_s, fin_r, fing_s, fing_r, in_s, out_s, off_s,
):
    k = lax.axis_index("tm")
    y = lax.axis_index("row")
    core = k % 2
    column = k // 2
    parity = y // 2
    e = 2 * column + parity
    first = y + parity * (3 - 2 * y)
    q = first + core * (3 - 2 * first)
    q_sib = 3 - q
    q_par = q + 1 - 2 * (q % 2)
    q_dia = 3 - q_par
    sib = (k + 1 - 2 * core, y)
    par = (k, y + 1 - 2 * (y % 2))
    stays = parity == core
    moves = parity != core
    partner = (k + 1 - 2 * core, 3 - y)

    def holder(element, quarter):
        c = quarter // 2
        b = quarter + c * (3 - 2 * quarter)
        p = element % 2
        return (2 * (element // 2) + c, b + p * (3 - 2 * b))

    def copy(src, dst, ssem, rsem, dev):
        return pltpu.make_async_remote_copy(
            src_ref=src, dst_ref=dst, send_sem=ssem, recv_sem=rsem, device_id=dev, device_id_type=MESH
        )

    def composes(el, s):
        return el + 2**s < steps

    def makes_gain(el, s):
        return el + 2 ** (s + 1) < steps

    def sends_gain(el, s):
        return jnp.logical_and(el >= 2**s, el + 2**s < steps)

    def both(a, b):
        return jnp.logical_and(a, b)

    feeds_self = both(core == 1, y < 2)

    barrier = pltpu.get_barrier_semaphore()

    def greet(dev):
        pl.semaphore_signal(barrier, inc=1, device_id=dev, device_id_type=MESH)

    greet(sib)
    greet(par)
    for row in range(4):

        @pl.when(jnp.logical_not(both(stays, row == y)))
        def _():
            greet((e, row))

        @pl.when(both(e + 1 < steps, jnp.logical_not(both(feeds_self, row == y))))
        def _():
            greet((e + 1, row))

    for s in range(1, levels):

        @pl.when(composes(e, s))
        def _():
            greet((k + 2**s, y))

    def count(flag):
        return flag.astype(jnp.int32)

    greetings = 2 + 4 - count(stays) + count(k >= 1) * (4 - count(feeds_self))
    for s in range(1, levels):
        greetings += count(e >= 2**s)

    def blocks(s):
        return e_first if s == 0 else e_later.at[s - 1]

    def gain(s, a, b):
        return e_first[a, b] if s == 0 else e_later[s - 1, b, a]

    parts = PARTS
    tiles = 4 // parts

    def half(s, blk, h):
        return blocks(s).at[blk, pl.ds(tiles * h, tiles)]

    def gain_sib(s, h):
        return copy(half(s, q, h), half(s, q, h), sib_s.at[s, h], sib_r.at[s, h], sib)

    def gain_sib_in(s, h):
        return copy(half(s, q_sib, h), half(s, q_sib, h), sib_s.at[s, h], sib_r.at[s, h], sib)

    def gain_par(s, h):
        return copy(half(s, q, h), half(s, q, h), par_s.at[s, h], par_r.at[s, h], par)

    def gain_par_in(s, h):
        return copy(half(s, q_par, h), half(s, q_par, h), par_s.at[s, h], par_r.at[s, h], par)

    def gain_fwd(s, h):
        return copy(half(s, q_par, h), half(s, q_par, h), fwd_s.at[s, h], fwd_r.at[s, h], sib)

    def gain_fwd_in(s, h):
        return copy(half(s, q_dia, h), half(s, q_dia, h), fwd_s.at[s, h], fwd_r.at[s, h], sib)

    def gain_start(s, h):
        gain_par(s, h).start()

    def far_gain(s, h):
        part = pl.ds(h * (4 // FARS), 4 // FARS)
        return copy(e_later.at[s - 1, q, part], far_e.at[s, part], fe_s.at[s, h], fe_r.at[s, h], (k - 2**s, y))

    def far_offset(s):
        return copy(own_g, far_g.at[s], fg_s.at[s], fg_r.at[s], (k - 2**s, y))

    pieces = 3 * HALVES

    def rows(c):
        return pl.ds(c % HALVES * (tile // HALVES), tile // HALVES)

    def far_tile(s, c):
        t = c // HALVES
        return copy(
            own_l.at[(q + t) % 4, rows(c)], far_l.at[s, 3 * q + t, rows(c)], lf_s.at[s, c], lf_r.at[s, c], (k - 2**s, y)
        )

    def tile_copy(s, c, owner, ssem, rsem, dev):
        ref = far_l.at[s, 3 * owner + c // HALVES, rows(c)]
        return copy(ref, ref, ssem.at[s, c], rsem.at[s, c], dev)

    def tile_sib(s, t):
        return tile_copy(s, t, q, ls_s, ls_r, sib)

    def tile_sib_in(s, t):
        return tile_copy(s, t, q_sib, ls_s, ls_r, sib)

    def tile_par(s, t):
        return tile_copy(s, t, q, lp_s, lp_r, par)

    def tile_par_in(s, t):
        return tile_copy(s, t, q_par, lp_s, lp_r, par)

    def tile_fwd(s, t):
        return tile_copy(s, t, q_par, lw_s, lw_r, sib)

    def tile_fwd_in(s, t):
        return tile_copy(s, t, q_dia, lw_s, lw_r, sib)

    def if_tile(t, whose, run):
        if t < 2 * HALVES:
            run()
        else:
            pl.when(whose == 0)(run)

    def spread(s, a, b):
        t = (b - a) % 4
        if t < 2 or (t == 2 and a < 2):
            return far_l[s, 3 * a + t], False
        return far_l[s, 3 * b + (4 - t)], True

    def move_gain(h):
        part = pl.ds(tiles * h, tiles)
        return copy(stage_e.at[part], e_first.at[y, part], mve_s.at[h], mve_r.at[h], partner)

    def move_gain_in(h):
        part = pl.ds(tiles * h, tiles)
        return copy(stage_e.at[part], e_first.at[q, part], mve_s.at[h], mve_r.at[h], partner)

    def move_spread():
        return copy(stage_l, own_l, mvl_s, mvl_r, partner)

    def gain_direct(quarter):
        return copy(
            stage_e.at[quarter], far_e.at[0, y], fed_s.at[quarter], fed_r.at[y], holder(k - 1, quarter)
        )

    def gain_direct_in(row):
        return copy(stage_e.at[0], far_e.at[0, row], fed_s.at[row], fed_r.at[row], sib)

    def tile_direct(c):
        t = c // HALVES
        return copy(
            stage_l.at[(y + t) % 4, rows(c)], far_l.at[0, 3 * y + t, rows(c)], lf_s.at[0, c], lf_r.at[0, c],
            holder(k - 1, y),
        )

    def tile_in(s, c):
        return copy(own_l.at[0, rows(c)], far_l.at[s, 3 * q + c // HALVES, rows(c)], lf_s.at[s, c], lf_r.at[s, c], sib)

    def offset_direct(quarter):
        return copy(stage_g, own_g.at[y], gd_s.at[quarter], gd_r.at[y], holder(k, quarter))

    def offset_direct_in(row):
        return copy(stage_g, own_g.at[row], gd_s.at[row], gd_r.at[row], sib)

    def offset_direct_far(quarter):
        return copy(stage_g, far_g.at[0, y], fgd_s.at[quarter], fgd_r.at[y], holder(k - 1, quarter))

    def offset_direct_far_in(row):
        return copy(stage_g, far_g.at[0, row], fgd_s.at[row], fgd_r.at[row], sib)

    def load_gain(n):
        return pltpu.make_async_copy(e_in.at[0, :, pl.ds(n * tile, tile)], stage_e.at[n], in_s.at[0, n])

    def load_own_gain(n):
        return pltpu.make_async_copy(e_in.at[0, :, pl.ds(n * tile, tile)], e_first.at[q, n], in_s.at[1, n])

    def load_spread(n):
        return pltpu.make_async_copy(l_in.at[0, :, pl.ds(n * tile, tile)], stage_l.at[n], in_s.at[2, n])

    def load_own_spread(n):
        return pltpu.make_async_copy(l_in.at[0, :, pl.ds(n * tile, tile)], own_l.at[n], in_s.at[3, n])

    def store_own(n):
        return pltpu.make_async_copy(own_l.at[n], o_l.at[0, :, pl.ds(pl.multiple_of(n * tile, tile), tile)], out_s.at[n])

    def store_back(n):
        return pltpu.make_async_copy(fin_l.at[n], o_l.at[0, :, pl.ds(pl.multiple_of(n * tile, tile), tile)], out_s.at[n])

    def back(n):
        return copy(own_l.at[n], fin_l.at[n], fin_s.at[n], fin_r.at[n], partner)

    def back_offset():
        return copy(own_g.at[q], fin_g, fing_s, fing_r, partner)

    input_gain_sent = both(k >= 1, makes_gain(k - 1, 0))

    for n in range(4):
        load_spread(n).start()
    for n in range(4):
        load_gain(n).start()

    @pl.when(stays)
    def _():
        for n in range(4):
            load_own_gain(n).start()
        for n in range(4):
            load_own_spread(n).start()

    load_offset = pltpu.make_async_copy(g_in, offset_row, off_s)
    load_offset.start()
    load_offset.wait()
    first_row = lax.broadcasted_iota(jnp.int32, (SLAB, tile), 0) == 0
    slab = jnp.broadcast_to(offset_row[...].astype(F32), (SLAB, tile))
    stage_g[...] = jnp.where(first_row, slab, 0.0).astype(BF16)
    for n in range(4):
        load_spread(n).wait()
    for n in range(4):
        load_gain(n).wait()

    @pl.when(stays)
    def _():
        for n in range(4):
            load_own_gain(n).wait()

    pl.semaphore_wait(barrier, greetings)

    @pl.when(both(moves, composes(k, 0)))
    def _():
        for h in range(parts):
            move_gain(h).start()

    @pl.when(both(stays, composes(e, 0)))
    def _():
        for h in range(parts):
            gain_start(0, h)
        for h in range(parts):
            gain_sib(0, h).start()

    @pl.when(stays)
    def _():
        for n in range(4):
            load_own_spread(n).wait()

    def ring_moved(s, h):
        @pl.when(both(moves, composes(e, s)))
        def _():
            move_gain_in(h).wait_recv()
            gain_start(s, h)
            gain_sib(s, h).start()

    def tiles_direct(s):
        @pl.when(k >= 1)
        def _():
            for c in range(pieces):
                if_tile(c, y // 2, lambda c=c: tile_direct(c).start())

    def offsets_out(s):
        for quarter in range(4):
            here = both(stays, quarter == y)

            @pl.when(jnp.logical_not(here))
            def _():
                offset_direct(quarter).start()

            @pl.when(here)
            def _():
                own_g[y] = stage_g[...]

        @pl.when(k >= 1)
        def _():
            for quarter in range(4):
                here = both(feeds_self, quarter == 3 - y)

                @pl.when(jnp.logical_not(here))
                def _():
                    offset_direct_far(quarter).start()

                @pl.when(here)
                def _():
                    far_g[0, y] = stage_g[...]

    def spread_out(s):
        @pl.when(moves)
        def _():
            move_spread().start()

    def direct_out(s):
        @pl.when(input_gain_sent)
        def _():
            for quarter in range(4):
                here = both(feeds_self, quarter == 3 - y)

                @pl.when(jnp.logical_not(here))
                def _():
                    gain_direct(quarter).start()

                @pl.when(here)
                def _():
                    far_e[0, y] = stage_e[quarter]

    def ring_out(s, h):
        @pl.when(composes(e, s))
        def _():
            gain_start(s, h)

    def ring_near(s):
        @pl.when(composes(e, s))
        def _():
            for h in range(parts):
                gain_sib(s, h).start()

    def far_out(s, h):
        @pl.when(sends_gain(e, s))
        def _():
            far_gain(s, h).start()

    def ring_on(s, h):
        @pl.when(composes(e, s))
        def _():
            gain_par_in(s, h).wait_recv()
            gain_fwd(s, h).start()

    def tile_on(s, t):
        def run():
            tile_in(s, t).wait_recv()
            tile_par(s, t).start()
            tile_sib(s, t).start()

        @pl.when(composes(e, s))
        def _():
            if_tile(t, core, run)

    def tile_over(s, t):
        def run():
            tile_par_in(s, t).wait_recv()
            tile_fwd(s, t).start()

        @pl.when(composes(e, s))
        def _():
            if_tile(t, core, run)

    def gain_beside(s):
        @pl.when(composes(e, s))
        def _():
            for h in range(parts):
                gain_sib_in(s, h).wait_recv()

    def gain_near(s):
        @pl.when(makes_gain(e, s))
        def _():
            if s == 0:
                for row in range(4):

                    @pl.when(jnp.logical_not(both(feeds_self, row == y)))
                    def _():
                        gain_direct_in(row).wait_recv()

            else:
                for h in range(FARS):
                    far_gain(s, h).wait_recv()
                for a in range(4):
                    acc_e[a] = (
                        dot(gain(s, a, q), far_e[s, q])
                        + dot(gain(s, a, q_sib), far_e[s, q_sib])
                        + dot(gain(s, a, q_par), far_e[s, q_par])
                    )

    def gain_whole(s):
        @pl.when(composes(e, s))
        def _():
            for h in range(parts):
                gain_fwd_in(s, h).wait_recv()

    def gain_new(s):
        @pl.when(makes_gain(e, s))
        def _():
            for a in range(4):
                if s == 0:
                    total = dot(gain(s, a, 0), far_e[s, 0])
                    for b in range(1, 4):
                        total += dot(gain(s, a, b), far_e[s, b])
                else:
                    total = acc_e[a] + dot(gain(s, a, q_dia), far_e[s, q_dia])
                e_later[s, q, a] = total.astype(BF16)

    def middle(s):
        @pl.when(composes(e, s))
        def _():
            for t in range(pieces):

                def run(t=t):
                    tile_sib_in(s, t).wait_recv()
                    tile_fwd_in(s, t).wait_recv()

                if_tile(t, 1 - core, run)
            for n in range(4):
                total = None
                for b in range(4):
                    part, turned = spread(s, b, n)
                    term = (dot_t if turned else dot)(gain(s, q, b), part)
                    total = term if total is None else total + term
                mid[n, pl.ds(0, tile), :] = total.astype(BF16)
            if s == 0:
                for row in range(4):

                    @pl.when(jnp.logical_not(both(feeds_self, row == y)))
                    def _():
                        offset_direct_far_in(row).wait_recv()

            else:
                copy(far_g.at[s], far_g.at[s], fg_s.at[s], fg_r.at[s], sib).wait_recv()
            for b in range(4):
                mid[b, pl.ds(tile, SLAB), :] = far_g[s, b]

    def spread_new(s):
        more = s + 1 < levels
        if s == 0:

            @pl.when(moves)
            def _():
                move_spread().wait_recv()

            for row in range(4):

                @pl.when(jnp.logical_not(both(stays, row == y)))
                def _():
                    offset_direct_in(row).wait_recv()

        else:

            @pl.when(e >= 2**s)
            def _():
                for t in range(pieces):
                    if_tile(t, core, lambda t=t: far_tile(s, t).wait_send())
                far_offset(s).wait_send()

        @pl.when(composes(e, s))
        def _():
            for o in range(4):
                n = (q + o) % 4
                total = dot_t(mid[0], gain(s, n, 0))
                for b in range(1, 4):
                    total += dot_t(mid[b], gain(s, n, b))
                own_l[n] = (total[0:tile] + own_l[n].astype(F32)).astype(BF16)
                own_g[n] = (total[tile:] + own_g[n].astype(F32)).astype(BF16)
                if more:
                    if o < 3:

                        @pl.when(e >= 2 ** (s + 1))
                        def _():
                            for c in range(HALVES * o, HALVES * (o + 1)):
                                if_tile(c, core, lambda c=c: far_tile(s + 1, c).start())

                else:

                    @pl.when(moves)
                    def _():
                        back(n).start()

                    @pl.when(stays)
                    def _():
                        store_own(n).start()

        if more:

            @pl.when(both(e >= 2 ** (s + 1), jnp.logical_not(composes(e, s))))
            def _():
                for t in range(pieces):
                    if_tile(t, core, lambda t=t: far_tile(s + 1, t).start())

            @pl.when(e >= 2 ** (s + 1))
            def _():
                far_offset(s + 1).start()

        else:

            @pl.when(both(moves, jnp.logical_not(composes(e, s))))
            def _():
                for n in range(4):
                    back(n).start()

            @pl.when(both(stays, jnp.logical_not(composes(e, s))))
            def _():
                for n in range(4):
                    store_own(n).start()

    steps_of = dict(
        B=ring_moved, D=direct_out, T=tiles_direct, P=spread_out, O=offsets_out, b=gain_beside, G=ring_out, H=ring_near, F=far_out, g=ring_on, t=tile_on, u=tile_over, n=gain_near, w=gain_whole, E=gain_new, M=middle,
        L=spread_new,
    )
    for word in PLAN:
        args = [int(digit) for digit in word[1:]]
        steps_of[word[0]](*args)

    @pl.when(moves)
    def _():
        back_offset().start()
        for o in range(4):
            n = (y + o) % 4
            copy(own_l.at[n], fin_l.at[n], fin_s.at[n], fin_r.at[n], partner).wait_recv()
            store_back(n).start()
        back_offset().wait_recv()
        o_g[...] = fin_g[0:1]

    @pl.when(stays)
    def _():
        o_g[...] = own_g[q][0:1]

    for n in range(4):
        store_own(n).wait()
    @pl.when(moves)
    def _():
        back_offset().wait_send()
        for n in range(4):
            back(n).wait_send()
        move_spread().wait_send()

    @pl.when(both(moves, composes(k, 0)))
    def _():
        for h in range(parts):
            move_gain(h).wait_send()

    for quarter in range(4):
        here = both(feeds_self, quarter == 3 - y)

        @pl.when(both(input_gain_sent, jnp.logical_not(here)))
        def _():
            gain_direct(quarter).wait_send()

        @pl.when(both(k >= 1, jnp.logical_not(here)))
        def _():
            offset_direct_far(quarter).wait_send()

        @pl.when(jnp.logical_not(both(stays, quarter == y)))
        def _():
            offset_direct(quarter).wait_send()

    @pl.when(k >= 1)
    def _():
        for t in range(pieces):
            if_tile(t, y // 2, lambda t=t: tile_direct(t).wait_send())

    for s in range(levels):

        @pl.when(composes(e, s))
        def _():
            for h in range(parts):
                gain_par(s, h).wait_send()
                gain_sib(s, h).wait_send()
                gain_fwd(s, h).wait_send()
            for t in range(pieces):

                def run(t=t):
                    tile_par(s, t).wait_send()
                    tile_sib(s, t).wait_send()
                    tile_fwd(s, t).wait_send()

                if_tile(t, core, run)

        if s > 0:

            @pl.when(sends_gain(e, s))
            def _():
                for h in range(FARS):
                    far_gain(s, h).wait_send()


def per_device(gain_mats, offsets, spread_mats):
    steps = lax.axis_size("tm")
    levels = steps.bit_length() - 1
    tile = gain_mats.shape[1]
    dma = pltpu.SemaphoreType.DMA
    flops = levels * 3 * 2 * tile * (4 * tile) ** 2
    square = (tile, tile)
    return pl.pallas_call(
        functools.partial(kernel, steps, levels, tile),
        name="scan",
        out_shape=(
            jax.ShapeDtypeStruct(offsets.shape, BF16),
            jax.ShapeDtypeStruct(spread_mats.shape, BF16),
        ),
        in_specs=[pl.BlockSpec(memory_space=pltpu.HBM)] * 3,
        out_specs=[pl.BlockSpec(memory_space=pltpu.VMEM)] * 2,
        scratch_shapes=[
            pltpu.VMEM((4, *square), BF16),
            pltpu.VMEM((4, *square), BF16),
            pltpu.VMEM((SLAB, tile), BF16),
            pltpu.VMEM((4, 4, *square), BF16),
            pltpu.VMEM((levels - 1, 4, 4, *square), BF16),
            pltpu.VMEM((levels - 1, 4, *square), BF16),
            pltpu.VMEM((levels, 12, *square), BF16),
            pltpu.VMEM((levels, 4, SLAB, tile), BF16),
            pltpu.VMEM((4, *square), BF16),
            pltpu.VMEM((4, SLAB, tile), BF16),
            pltpu.VMEM((4, tile + SLAB, tile), BF16),
            pltpu.VMEM((4, *square), F32),
            pltpu.VMEM((4, *square), BF16),
            pltpu.VMEM((SLAB, tile), BF16),
            pltpu.VMEM((1, tile), BF16),
            dma((4,)), dma((4,)), dma, dma,
            dma((4,)), dma((4,)), dma((levels, 4)), dma((levels, 4)),
            dma((4,)), dma((4,)), dma((4,)), dma((4,)), dma((levels,)), dma((levels,)),
            dma((levels, 4)), dma((levels, 4)), dma((levels, 4)), dma((levels, 4)), dma((levels, 4)), dma((levels, 4)),
            dma((levels, 6)), dma((levels, 6)), dma((levels, 6)), dma((levels, 6)),
            dma((levels, 6)), dma((levels, 6)), dma((levels, 6)), dma((levels, 6)),
            dma((4,)), dma((4,)), dma, dma,
            dma((4, 4)), dma((4,)), dma,
        ],
        compiler_params=pltpu.CompilerParams(
            collective_id=0, has_side_effects=True, vmem_limit_bytes=40 * 2**20
        ),
        cost_estimate=pl.CostEstimate(flops=flops, bytes_accessed=3 * tile * 4 * tile * 2, transcendentals=0),
    )(gain_mats, offsets, spread_mats)


def solution(mesh):
    in_specs = (P("tm", "row", None), P("tm", "row"), P("tm", "row", None))
    out_specs = (P("tm", "row"), P("tm", "row", None))
    return jax.shard_map(per_device, mesh=mesh, in_specs=in_specs, out_specs=out_specs, check_vma=False)
```

time: 147 us -> 137 us (0.932)
  Pallas kernels: 142 us -> 132 us
    pallas_call x1, Pallas kernels: 142 us -> 132 us  [per_device(): pl.pallas_call(functools.partial(kernel, steps, levels, tile), name='scan...]
where the time goes in v4:
time: 137 us
  Pallas kernels  132 us (96%)
  local copies, waits for them, and re-layouts  4.11 us (3%)
    pallas_call x1, Pallas kernels, per_device(): pl.pallas_call(functools.partial(kernel, steps, levels, tile), name='scan...  132 us
    unnamed x8, local copies, waits for them, and re-layouts  4.11 us

profile of v4, /device:TPU:3, one launch (start us, length us, event | category | flops | bytes accessed | tf_op | source)
XLA Modules:
  0.0 136.9 jit_solution(929081206083116538)
XLA Ops:
  0.6 0.0 copy-start
  0.6 1.0 copy-done
  1.7 0.0 copy-start.1
  1.7 1.0 copy-done.1
  2.7 0.0 copy-start.2
  2.7 0.7 copy-done.2
  3.4 132.1 %scan.1 = (bf16[1,256]{1,0:T(2,128)(2,1)S(1)}, bf16[1,256,1024]{2,1,0:T(8,128)(2,1)S(1)}) custom-call(bf16[1,256,1024]{2,1,0:T(8,128)(2,1)S(1)} %copy-done, bf16[1,256]{1,0:T(2,128)(2,1)S(1)} %copy-done.2, bf16[1,256,1024]{2,1,0:T(8,128)(2,1)S(1)} %copy-done.1), custom_call_target="tpu_custom_call" | custom-call | flops 8053063680 | bytes 1572864 | tf_op jit(solution)/shard_map/scan/pallas_call | solution.py:646
  135.5 0.6 copy.7
  136.1 0.8 copy.8
Async XLA Ops:
  0.6 1.0 copy-start
  1.7 1.0 copy-start.1
  2.7 0.7 copy-start.2

commit v5 on v4

--- a/solution.py
+++ b/solution.py
@@ -11,16 +11,15 @@
 BF16 = jnp.bfloat16
 F32 = jnp.float32
 PLAN = (
-    "D0", "T0", "P0", "O0", "B00", "B01", "g00", "t00", "t01", "g01", "b0", "n0", "w0", "E0", "F10", "F11", "F12", "F13", "H1", "t02",
-    "t03", "t04", "t05", "G10", "G11", "u00", "u01", "u02", "u03", "u04", "u05", "M0", "L0", "g10", "t10", "t11", "g11", "b1", "n1", "w1",
-    "E1", "F20", "F21", "F22", "F23", "H2", "t12", "t13", "t14", "t15", "G20", "G21", "u10", "u11", "u12", "u13", "u14", "u15", "M1", "L1",
-    "g20", "t20", "t21", "g21", "b2", "n2", "w2", "E2", "F30", "F31", "F32", "F33", "H3", "t22", "t23", "t24", "t25", "G30", "G31", "u20",
-    "u21", "u22", "u23", "u24", "u25", "M2", "L2", "g30", "t30", "t31", "g31", "b3", "n3", "w3", "E3", "F40", "F41", "F42", "F43", "H4",
-    "t32", "t33", "t34", "t35", "G40", "G41", "u30", "u31", "u32", "u33", "u34", "u35", "M3", "L3", "g40", "t40", "t41", "g41", "b4", "w4",
-    "t42", "t43", "t44", "t45", "u40", "u41", "u42", "u43", "u44", "u45", "M4", "L4",
+    "D0", "T0", "P0", "O0", "B00", "B01", "g00", "t00", "t01", "b0", "g01", "n0", "t02", "w0", "E0", "F10", "H1", "t03", "t04", "t05",
+    "G10", "G11", "u00", "u01", "u02", "u03", "u04", "u05", "M0", "L0", "g10", "t10", "t11", "b1", "g11", "n1", "t12", "w1", "E1", "F20",
+    "H2", "t13", "t14", "t15", "G20", "G21", "u10", "u11", "u12", "u13", "u14", "u15", "M1", "L1", "g20", "t20", "t21", "b2", "g21", "n2",
+    "t22", "w2", "E2", "F30", "H3", "t23", "t24", "t25", "G30", "G31", "u20", "u21", "u22", "u23", "u24", "u25", "M2", "L2", "g30", "t30",
+    "t31", "b3", "g31", "n3", "t32", "w3", "E3", "F40", "H4", "t33", "t34", "t35", "G40", "G41", "u30", "u31", "u32", "u33", "u34", "u35",
+    "M3", "L3", "g40", "t40", "t41", "b4", "g41", "t42", "w4", "t43", "t44", "t45", "u40", "u41", "u42", "u43", "u44", "u45", "M4", "L4",
 )
 HALVES = 2
-FARS = 4
+FARS = 1
 PARTS = 2
 SLAB = 16
 
@@ -658,7 +657,7 @@
             pltpu.VMEM((SLAB, tile), BF16),
             pltpu.VMEM((4, 4, *square), BF16),
             pltpu.VMEM((levels - 1, 4, 4, *square), BF16),
-            pltpu.VMEM((levels - 1, 4, *square), BF16),
+            pltpu.VMEM((levels, 4, *square), BF16),
             pltpu.VMEM((levels, 12, *square), BF16),
             pltpu.VMEM((levels, 4, SLAB, tile), BF16),
             pltpu.VMEM((4, *square), BF16),

time: 137 us -> 137 us (level)
  no operation moved by 1% of the time
where the time goes in v5:
time: 137 us; the launch traced here: 136 us
  Pallas kernels  131 us (96%)
  local copies, waits for them, and re-layouts  4.11 us (3%)
    pallas_call x1, Pallas kernels, per_device(): pl.pallas_call(functools.partial(kernel, steps, levels, tile), name='scan...  131 us
    unnamed x8, local copies, waits for them, and re-layouts  4.11 us

profile of v5, /device:TPU:3, one launch (start us, length us, event | category | flops | bytes accessed | tf_op | source)
XLA Modules:
  0.0 135.9 jit_solution(10443904355512018837)
XLA Ops:
  0.6 0.0 copy-start
  0.6 1.0 copy-done
  1.7 0.0 copy-start.1
  1.7 1.0 copy-done.1
  2.7 0.0 copy-start.2
  2.7 0.7 copy-done.2
  3.4 131.1 %scan.1 = (bf16[1,256]{1,0:T(2,128)(2,1)S(1)}, bf16[1,256,1024]{2,1,0:T(8,128)(2,1)S(1)}) custom-call(bf16[1,256,1024]{2,1,0:T(8,128)(2,1)S(1)} %copy-done, bf16[1,256]{1,0:T(2,128)(2,1)S(1)} %copy-done.2, bf16[1,256,1024]{2,1,0:T(8,128)(2,1)S(1)} %copy-done.1), custom_call_target="tpu_custom_call" | custom-call | flops 8053063680 | bytes 1572864 | tf_op jit(solution)/shard_map/scan/pallas_call | solution.py:645
  134.5 0.6 copy.7
  135.1 0.8 copy.8
Async XLA Ops:
  0.6 1.0 copy-start
  1.7 1.0 copy-start.1
  2.7 0.7 copy-start.2

commit v6 on v5

--- a/solution.py
+++ b/solution.py
@@ -15,8 +15,8 @@
     "G10", "G11", "u00", "u01", "u02", "u03", "u04", "u05", "M0", "L0", "g10", "t10", "t11", "b1", "g11", "n1", "t12", "w1", "E1", "F20",
     "H2", "t13", "t14", "t15", "G20", "G21", "u10", "u11", "u12", "u13", "u14", "u15", "M1", "L1", "g20", "t20", "t21", "b2", "g21", "n2",
     "t22", "w2", "E2", "F30", "H3", "t23", "t24", "t25", "G30", "G31", "u20", "u21", "u22", "u23", "u24", "u25", "M2", "L2", "g30", "t30",
-    "t31", "b3", "g31", "n3", "t32", "w3", "E3", "F40", "H4", "t33", "t34", "t35", "G40", "G41", "u30", "u31", "u32", "u33", "u34", "u35",
-    "M3", "L3", "g40", "t40", "t41", "b4", "g41", "t42", "w4", "t43", "t44", "t45", "u40", "u41", "u42", "u43", "u44", "u45", "M4", "L4",
+    "t31", "b3", "g31", "n3", "t32", "w3", "E3", "H4", "t33", "t34", "t35", "G40", "G41", "u30", "u31", "u32", "u33", "u34", "u35", "M3",
+    "L3", "t40", "t41", "t42", "t43", "g40", "t44", "t45", "g41", "u40", "u41", "u42", "u43", "u44", "u45", "b4", "w4", "M4", "L4",
 )
 HALVES = 2
 FARS = 1

time: 137 us -> 136 us (level)
  no operation moved by 1% of the time
where the time goes in v6:
time: 136 us
  Pallas kernels  131 us (96%)
  local copies, waits for them, and re-layouts  4.11 us (3%)
    pallas_call x1, Pallas kernels, per_device(): pl.pallas_call(functools.partial(kernel, steps, levels, tile), name='scan...  131 us
    unnamed x8, local copies, waits for them, and re-layouts  4.11 us

profile of v6, /device:TPU:3, one launch (start us, length us, event | category | flops | bytes accessed | tf_op | source)
XLA Modules:
  0.0 135.9 jit_solution(11860518915247632098)
XLA Ops:
  0.6 0.0 copy-start
  0.6 1.0 copy-done
  1.7 0.0 copy-start.1
  1.7 1.0 copy-done.1
  2.7 0.0 copy-start.2
  2.7 0.7 copy-done.2
  3.4 131.1 %scan.1 = (bf16[1,256]{1,0:T(2,128)(2,1)S(1)}, bf16[1,256,1024]{2,1,0:T(8,128)(2,1)S(1)}) custom-call(bf16[1,256,1024]{2,1,0:T(8,128)(2,1)S(1)} %copy-done, bf16[1,256]{1,0:T(2,128)(2,1)S(1)} %copy-done.2, bf16[1,256,1024]{2,1,0:T(8,128)(2,1)S(1)} %copy-done.1), custom_call_target="tpu_custom_call" | custom-call | flops 8053063680 | bytes 1572864 | tf_op jit(solution)/shard_map/scan/pallas_call | solution.py:645
  134.5 0.6 copy.7
  135.1 0.8 copy.8
Async XLA Ops:
  0.6 1.0 copy-start
  1.7 1.0 copy-start.1
  2.7 0.7 copy-start.2
